TPU v7x, 128 devices: a whole 4x4x4 slice. The times are simulated.
128 devices in a mesh: row: 16 (over z, y), col: 8 (over x, core).
Axes of the slice: x: 4, y: 4, z: 4, core: 2. Of those that a mesh axis runs over, the one named last changes fastest.
Arguments:
- inputs: bfloat16 [256, 16384], P('col', 'row'), may hold values from -6 to 6
- grad_out: bfloat16 [256, 16384], P('col', 'row'), may hold values from -6 to 6
- gate_blocks: bfloat16 [16, 8, 96, 128, 128], P('row', 'col'), may hold values from -0.09375 to 0.09375
- up_blocks: bfloat16 [16, 8, 96, 128, 128], P('row', 'col'), may hold values from -0.09375 to 0.09375
- down_blocks: bfloat16 [16, 8, 96, 128, 128], P('row', 'col'), may hold values from -0.078125 to 0.078125
- gate_slots: int32 [16, 8, 96], P('row', 'col'), may hold values from 0 to 207, as said below
- gate_count: int32 [16, 8], P('row', 'col'), may hold values from 12 to 96, as said below
- down_slots: int32 [16, 8, 96], P('row', 'col'), may hold values from 0 to 207, as said below
- down_count: int32 [16, 8], P('row', 'col'), may hold values from 12 to 96, as said below
Outputs:
- layer_out: bfloat16 [256, 16384], P('col', 'row')
- grad_x: bfloat16 [256, 16384], P('col', 'row')
- grad_gate_blocks: bfloat16 [16, 8, 96, 128, 128], P('row', 'col')
- grad_up_blocks: bfloat16 [16, 8, 96, 128, 128], P('row', 'col')
- grad_down_blocks: bfloat16 [16, 8, 96, 128, 128], P('row', 'col')
Inputs may be any that keep to these rules, and one draw needn't show every extreme that they name: `gate_slots`: the 96 entries of one device are distinct positions in its 8 x 26 grid of blocks. `down_slots`: the 96 entries of one device are distinct positions in its 8 x 26 grid of blocks. `gate_count`: some device has all 96 slots live. `down_count`: some device has all 96 slots live.
All inputs are finite; a program needn't handle non-finite values.
Results may differ from a plain program's by a relative error of at most 0.03.
Values may be sent and summed in bfloat16 or wider, within the bound.
A program may use at most 192 MiB of HBM per device.

v0:
```python
import jax
import jax.numpy as jnp
from jax import lax
from jax.experimental import pallas as pl
from jax.experimental.pallas import tpu as pltpu
from jax.sharding import PartitionSpec as P

TOKENS = 256
BLOCK = 128
NB = 96
DPB = 8
FPB = 26
WIDTH = DPB * BLOCK
CHUNK = 2 * BLOCK
CHUNKS = FPB // 2
GROUP = 8
MESH = pl.DeviceIdType.MESH
F32 = jnp.float32
BF16 = jnp.bfloat16


def nt_dot(a, b):
    return lax.dot_general(a, b, (((1,), (1,)), ((), ())), preferred_element_type=F32)


def layer_kernel(
    gate_at,
    down_at,
    x_in,
    cot_in,
    gate_in,
    up_in,
    down_in,
    out_ref,
    gradx_ref,
    acts_out,
    xs_out,
    xs,
    raw_gate,
    raw_up,
    raw_down,
    w_gate,
    w_up,
    w_down,
    terms,
    half_al,
    half_ar,
    full_al,
    full_ar,
    sums,
    half_bl,
    half_br,
    full_bl,
    full_br,
    acts,
    out_acc,
    gradx_acc,
    tail,
    tail_core,
    tail_hl,
    tail_hr,
    tail_fl,
    tail_fr,
    load_sem,
    save_sem,
    head_send,
    head_recv,
    send_sem,
    recv_sem,
    tail_send,
    tail_recv,
):
    row, col = lax.axis_index("row"), lax.axis_index("col")
    z, y = row // 4, row % 4
    ix, core = col // 2, col % 2

    def y_dev(step):
        return (z * 4 + (y + step) % 4, col)

    def z_dev(step):
        return (((z + step) % 4) * 4 + y, col)

    def x_dev(step):
        return (row, ((ix + step) % 4) * 2 + core)

    sibling = (row, ix * 2 + 1 - core)

    loads = [
        pltpu.make_async_copy(x_in, xs.at[col, 0], load_sem.at[0]),
        pltpu.make_async_copy(cot_in, xs.at[col, 1], load_sem.at[1]),
        pltpu.make_async_copy(gate_in, raw_gate.at[pl.ds(0, NB)], load_sem.at[2]),
        pltpu.make_async_copy(up_in, raw_up.at[pl.ds(0, NB)], load_sem.at[3]),
        pltpu.make_async_copy(down_in, raw_down.at[pl.ds(0, NB)], load_sem.at[4]),
    ]
    for load in loads:
        load.start()

    barrier = pltpu.get_barrier_semaphore()
    for dev in (y_dev(1), y_dev(3), z_dev(1), z_dev(3), x_dev(1), x_dev(3), sibling):
        pl.semaphore_signal(barrier, inc=1, device_id=dev, device_id_type=MESH)

    zero = jnp.zeros((BLOCK, BLOCK), BF16)
    raw_gate[NB] = zero
    raw_up[NB] = zero
    raw_down[NB] = zero
    out_acc[...] = jnp.zeros_like(out_acc)
    gradx_acc[...] = jnp.zeros_like(gradx_acc)

    loads[0].wait()
    loads[1].wait()
    pl.semaphore_wait(barrier, 7)

    def head(n, ref, dev):
        return pltpu.make_async_remote_copy(
            src_ref=ref,
            dst_ref=ref,
            send_sem=head_send.at[n],
            recv_sem=head_recv.at[n],
            device_id=dev,
            device_id_type=MESH,
        )

    def at_x(step, side):
        return ((ix + step) % 4) * 2 + side

    other = 1 - core
    sent = []

    def head_start(n, ref, dev):
        copy = head(n, ref, dev)
        copy.start()
        sent.append(copy)

    head_start(0, xs.at[col], x_dev(1))
    head_start(1, xs.at[col], x_dev(3))
    head_start(2, xs.at[col], sibling)

    def place_gate(k, carry):
        for raw, dense in ((raw_gate, w_gate), (raw_up, w_up)):
            for r in range(DPB):
                for b in range(2):
                    slot = gate_at[r * FPB + 2 * k + b]
                    dense[k, r * BLOCK : (r + 1) * BLOCK, b * BLOCK : (b + 1) * BLOCK] = raw[slot]
        return carry

    def place_down(k, carry):
        for r in range(DPB):
            for b in range(2):
                slot = down_at[r * FPB + 2 * k + b]
                w_down[k, b * BLOCK : (b + 1) * BLOCK, r * BLOCK : (r + 1) * BLOCK] = raw_down[slot]
        return carry

    loads[2].wait()
    loads[3].wait()
    lax.fori_loop(0, 6, place_gate, 0)

    head(0, xs.at[at_x(3, core)], x_dev(1)).wait_recv()
    head_start(3, xs.at[at_x(3, core), 0], x_dev(1))
    head_start(4, xs.at[at_x(3, core)], sibling)
    head(1, xs.at[at_x(1, core)], x_dev(3)).wait_recv()
    head_start(5, xs.at[at_x(1, core), 1], x_dev(3))
    head_start(6, xs.at[at_x(1, core)], sibling)

    lax.fori_loop(6, CHUNKS, place_gate, 0)

    head(3, xs.at[at_x(2, core), 0], x_dev(1)).wait_recv()
    head_start(7, xs.at[at_x(2, core), 0], sibling)
    head(5, xs.at[at_x(2, core), 1], x_dev(3)).wait_recv()
    head_start(8, xs.at[at_x(2, core), 1], sibling)

    loads[4].wait()
    lax.fori_loop(0, CHUNKS, place_down, 0)

    head(2, xs.at[at_x(0, other)], sibling).wait_recv()
    head(4, xs.at[at_x(3, other)], sibling).wait_recv()
    head(6, xs.at[at_x(1, other)], sibling).wait_recv()
    head(7, xs.at[at_x(2, other), 0], sibling).wait_recv()
    head(8, xs.at[at_x(2, other), 1], sibling).wait_recv()
    save_xs = pltpu.make_async_copy(xs, xs_out, save_sem.at[CHUNKS])
    save_xs.start()

    def places(k):
        odd = k % 2
        i = (1 - odd) * y + odd * z
        j = (1 - odd) * z + odd * y

        def dev(step, along_z):
            y_new = (y + (1 - along_z) * step) % 4
            z_new = (z + along_z * step) % 4
            return (z_new * 4 + y_new, col)

        return i, j, dev(1, odd), dev(3, odd), dev(1, 1 - odd), dev(3, 1 - odd)

    def copy(k, n, src, dst, dev):
        return pltpu.make_async_remote_copy(
            src_ref=src,
            dst_ref=dst,
            send_sem=send_sem.at[k, n],
            recv_sem=recv_sem.at[k, n],
            device_id=dev,
            device_id_type=MESH,
        )

    def all_copies(k):
        i, j, ar, al, br, bl = places(k)
        i1, i2, i3 = (i + 1) % 4, (i + 2) % 4, (i + 3) % 4
        j1, j2, j3 = (j + 1) % 4, (j + 2) % 4, (j + 3) % 4
        same = lambda n, ref, dev: copy(k, n, ref, ref, dev)
        return [
            lambda: copy(k, 0, terms.at[k, i2, 0], half_al.at[k], ar),
            lambda: copy(k, 1, terms.at[k, i2, 1], half_ar.at[k], al),
            lambda: copy(k, 2, terms.at[k, i1], full_al.at[k], ar),
            lambda: copy(k, 3, terms.at[k, i3], full_ar.at[k], al),
            lambda: copy(k, 4, sums.at[k, j2, 0], half_bl.at[k], br),
            lambda: copy(k, 5, sums.at[k, j2, 1], half_br.at[k], bl),
            lambda: copy(k, 6, sums.at[k, j1], full_bl.at[k], br),
            lambda: copy(k, 7, sums.at[k, j3], full_br.at[k], bl),
            lambda: same(8, acts.at[k, i, j], br),
            lambda: same(9, acts.at[k, i, j], bl),
            lambda: same(10, acts.at[k, i, j3, 0], br),
            lambda: same(11, acts.at[k, i, j1, 1], bl),
            lambda: same(12, acts.at[k, i], ar),
            lambda: same(13, acts.at[k, i], al),
            lambda: same(14, acts.at[k, i3, pl.ds(0, 2)], ar),
            lambda: same(15, acts.at[k, i1, pl.ds(2, 2)], al),
        ]

    def arrived(k, n, ref):
        i, j, ar, al, br, bl = places(k)
        copy(k, n, ref, ref, ar).wait_recv()

    def plus(a, b):
        return (a.astype(F32) + b.astype(F32)).astype(BF16)

    def p0(k):
        for part, (arr, weights) in enumerate(((0, w_gate), (0, w_up), (1, w_down))):
            if part < 2:
                lhs = xs[:, 0].reshape(TOKENS, WIDTH)
                val = jnp.dot(lhs, weights[k], preferred_element_type=F32)
            else:
                lhs = xs[:, 1].reshape(TOKENS, WIDTH)
                val = nt_dot(lhs, weights[k])
            val = val.astype(BF16)
            for b in range(2):
                terms[k, :, b, :, part * 16 : (part + 1) * 16, :] = val[
                    :, b * BLOCK : (b + 1) * BLOCK
                ].reshape(4, 4, 16, BLOCK)
        copies = all_copies(k)
        copies[0]().start()
        copies[1]().start()

    def p1(k):
        i, j, *_ = places(k)
        i1, i3 = (i + 1) % 4, (i + 3) % 4
        copies = all_copies(k)
        arrived(k, 0, half_al.at[k])
        terms[k, i1, 0] = plus(terms[k, i1, 0], half_al[k])
        copies[2]().start()
        arrived(k, 1, half_ar.at[k])
        terms[k, i3, 1] = plus(terms[k, i3, 1], half_ar[k])
        copies[3]().start()

    def p2(k):
        i, j, *_ = places(k)
        copies = all_copies(k)
        arrived(k, 2, full_al.at[k])
        arrived(k, 3, full_ar.at[k])
        for b in range(2):
            total = terms[k, i, b].astype(F32) + full_al[k, b].astype(F32)
            sums[k, :, b] = (total + full_ar[k, b].astype(F32)).astype(BF16)
        copies[4]().start()
        copies[5]().start()

    def p3(k):
        i, j, *_ = places(k)
        j1, j3 = (j + 1) % 4, (j + 3) % 4
        copies = all_copies(k)
        arrived(k, 4, half_bl.at[k])
        sums[k, j1, 0] = plus(sums[k, j1, 0], half_bl[k])
        copies[6]().start()
        arrived(k, 5, half_br.at[k])
        sums[k, j3, 1] = plus(sums[k, j3, 1], half_br[k])
        copies[7]().start()

    def p4(k):
        i, j, *_ = places(k)
        copies = all_copies(k)
        arrived(k, 6, full_bl.at[k])
        arrived(k, 7, full_br.at[k])
        total = sums[k, j].astype(F32) + full_bl[k].astype(F32) + full_br[k].astype(F32)
        gate, up, grad = total[:, 0:16], total[:, 16:32], total[:, 32:48]
        sigma = 1.0 / (1.0 + jnp.exp(-gate))
        acts[k, i, j, :, 0:16, :] = (gate * sigma * up).astype(BF16)
        acts[k, i, j, :, 16:32, :] = (grad * up * sigma * (1.0 + gate * (1.0 - sigma))).astype(BF16)
        acts[k, i, j, :, 32:48, :] = (grad * gate * sigma).astype(BF16)
        copies[8]().start()
        copies[9]().start()

    def p5(k):
        i, j, *_ = places(k)
        copies = all_copies(k)
        arrived(k, 8, acts.at[k, i, (j + 3) % 4])
        copies[10]().start()
        arrived(k, 9, acts.at[k, i, (j + 1) % 4])
        copies[11]().start()

    def p6(k):
        i, j, *_ = places(k)
        copies = all_copies(k)
        arrived(k, 10, acts.at[k, i, (j + 2) % 4, 0])
        arrived(k, 11, acts.at[k, i, (j + 2) % 4, 1])
        copies[12]().start()
        copies[13]().start()

    def p7(k):
        i, j, *_ = places(k)
        copies = all_copies(k)
        arrived(k, 12, acts.at[k, (i + 3) % 4])
        copies[14]().start()
        arrived(k, 13, acts.at[k, (i + 1) % 4])
        copies[15]().start()

    def p8(k):
        i, j, *_ = places(k)
        arrived(k, 14, acts.at[k, (i + 2) % 4, pl.ds(0, 2)])
        arrived(k, 15, acts.at[k, (i + 2) % 4, pl.ds(2, 2)])
        pltpu.make_async_copy(acts.at[k], acts_out.at[k], save_sem.at[k]).start()

        def act(part):
            cols = [
                acts[k, :, :, b, part * 16 : (part + 1) * 16, :].reshape(TOKENS, BLOCK)
                for b in range(2)
            ]
            return jnp.concatenate(cols, axis=1)

        hidden, grad_gate, grad_up = act(0), act(1), act(2)
        for n in range(4):
            cols = slice(n * 256, (n + 1) * 256)
            out_acc[:, cols] += jnp.dot(hidden, w_down[k, :, cols], preferred_element_type=F32)
            gradx_acc[:, cols] += nt_dot(grad_gate, w_gate[k, cols, :]) + nt_dot(
                grad_up, w_up[k, cols, :]
            )
        for one in all_copies(k):
            one().wait_send()

    def tick(t, carry):
        for phase, late in ((p7, 7), (p6, 6), (p5, 5), (p4, 4), (p3, 3), (p2, 2), (p1, 1), (p0, 0), (p8, 8)):
            k = t - late

            @pl.when(jnp.logical_and(k >= 0, k < CHUNKS))
            def _():
                phase(k)

        return carry

    lax.fori_loop(0, CHUNKS + 8, tick, 0)

    for side in range(2):
        for at in range(4):
            rows = slice((at * 2 + side) * 32, (at * 2 + side + 1) * 32)
            tail[side, at, 0] = out_acc[rows, :].astype(BF16)
            tail[side, at, 1] = gradx_acc[rows, :].astype(BF16)

    def last(n, src, dst, dev):
        return pltpu.make_async_remote_copy(
            src_ref=src,
            dst_ref=dst,
            send_sem=tail_send.at[n],
            recv_sem=tail_recv.at[n],
            device_id=dev,
            device_id_type=MESH,
        )

    x0, x1, x2, x3 = ix, (ix + 1) % 4, (ix + 2) % 4, (ix + 3) % 4
    cores = {
        n: last(n, tail.at[other, at], tail_core.at[at], sibling)
        for n, at in ((0, x2), (1, x1), (2, x3), (3, x0))
    }
    for n in range(4):
        cores[n].start()
    right, left = x_dev(1), x_dev(3)
    cores[0].wait_recv()
    tail[core, x2] = plus(tail[core, x2], tail_core[x2])
    halves = [last(4, tail.at[core, x2, 0], tail_hl, right), last(5, tail.at[core, x2, 1], tail_hr, left)]
    for half in halves:
        half.start()
    cores[1].wait_recv()
    tail[core, x1] = plus(tail[core, x1], tail_core[x1])
    cores[2].wait_recv()
    tail[core, x3] = plus(tail[core, x3], tail_core[x3])
    fulls = [last(6, tail.at[core, x1], tail_fl, right), last(7, tail.at[core, x3], tail_fr, left)]
    halves[0].wait_recv()
    tail[core, x1, 0] = plus(tail[core, x1, 0], tail_hl[...])
    fulls[0].start()
    halves[1].wait_recv()
    tail[core, x3, 1] = plus(tail[core, x3, 1], tail_hr[...])
    fulls[1].start()
    cores[3].wait_recv()
    total = tail[core, x0].astype(F32) + tail_core[x0].astype(F32)
    fulls[0].wait_recv()
    fulls[1].wait_recv()
    total = total + tail_fl[...].astype(F32) + tail_fr[...].astype(F32)
    out_ref[...] = total[0].astype(BF16)
    gradx_ref[...] = total[1].astype(BF16)

    for one in sent + list(cores.values()) + halves + fulls:
        one.wait_send()
    save_xs.wait()

    def saved(k, carry):
        pltpu.make_async_copy(acts.at[k], acts_out.at[k], save_sem.at[k]).wait()
        return carry

    lax.fori_loop(0, CHUNKS, saved, 0)


def run_layer(gate_at, down_at, inputs, grad_out, gate_blocks, up_blocks, down_blocks):
    anywhere = pl.BlockSpec(memory_space=pl.ANY)
    scalars = pl.BlockSpec(memory_space=pltpu.SMEM)
    vmem = pl.BlockSpec(memory_space=pltpu.VMEM)
    raw = pltpu.VMEM((NB + 1, BLOCK, BLOCK), BF16)
    part = (48, BLOCK)
    return pl.pallas_call(
        layer_kernel,
        out_shape=(
            jax.ShapeDtypeStruct((32, WIDTH), BF16),
            jax.ShapeDtypeStruct((32, WIDTH), BF16),
            jax.ShapeDtypeStruct((CHUNKS, 4, 4, 2) + part, BF16),
            jax.ShapeDtypeStruct((8, 2, 32, WIDTH), BF16),
        ),
        in_specs=[scalars, scalars] + [anywhere] * 5,
        out_specs=(vmem, vmem, anywhere, anywhere),
        scratch_shapes=[
            pltpu.VMEM((8, 2, 32, WIDTH), BF16),
            raw,
            raw,
            raw,
            pltpu.VMEM((CHUNKS, WIDTH, CHUNK), BF16),
            pltpu.VMEM((CHUNKS, WIDTH, CHUNK), BF16),
            pltpu.VMEM((CHUNKS, CHUNK, WIDTH), BF16),
            pltpu.VMEM((CHUNKS, 4, 2, 4) + part, BF16),
            pltpu.VMEM((CHUNKS, 4) + part, BF16),
            pltpu.VMEM((CHUNKS, 4) + part, BF16),
            pltpu.VMEM((CHUNKS, 2, 4) + part, BF16),
            pltpu.VMEM((CHUNKS, 2, 4) + part, BF16),
            pltpu.VMEM((CHUNKS, 4, 2) + part, BF16),
            pltpu.VMEM((CHUNKS,) + part, BF16),
            pltpu.VMEM((CHUNKS,) + part, BF16),
            pltpu.VMEM((CHUNKS, 2) + part, BF16),
            pltpu.VMEM((CHUNKS, 2) + part, BF16),
            pltpu.VMEM((CHUNKS, 4, 4, 2) + part, BF16),
            pltpu.VMEM((TOKENS, WIDTH), F32),
            pltpu.VMEM((TOKENS, WIDTH), F32),
            pltpu.VMEM((2, 4, 2, 32, WIDTH), BF16),
            pltpu.VMEM((4, 2, 32, WIDTH), BF16),
            pltpu.VMEM((32, WIDTH), BF16),
            pltpu.VMEM((32, WIDTH), BF16),
            pltpu.VMEM((2, 32, WIDTH), BF16),
            pltpu.VMEM((2, 32, WIDTH), BF16),
            pltpu.SemaphoreType.DMA((5,)),
            pltpu.SemaphoreType.DMA((CHUNKS + 1,)),
            pltpu.SemaphoreType.DMA((9,)),
            pltpu.SemaphoreType.DMA((9,)),
            pltpu.SemaphoreType.DMA((CHUNKS, 16)),
            pltpu.SemaphoreType.DMA((CHUNKS, 16)),
            pltpu.SemaphoreType.DMA((8,)),
            pltpu.SemaphoreType.DMA((8,)),
        ],
        compiler_params=pltpu.CompilerParams(
            collective_id=0, has_side_effects=True, vmem_limit_bytes=60 * 2**20
        ),
        name="layer",
    )(gate_at, down_at, inputs, grad_out, gate_blocks, up_blocks, down_blocks)


def grads_kernel(
    gate_slots, down_slots, counts, acts, xs, gate_out, up_out, down_out, x_t, cots, pairs, hidden_t
):
    step = pl.program_id(0)

    @pl.when(step == 0)
    def _():
        for r in range(DPB):
            cols = slice(r * BLOCK, (r + 1) * BLOCK)
            x_t[r] = xs[:, 0, :, cols].reshape(TOKENS, BLOCK).T
            cots[r] = xs[:, 1, :, cols].reshape(TOKENS, BLOCK)

        def relay(k, carry):
            for b in range(2):
                act = [
                    acts[k, :, :, b, part * 16 : (part + 1) * 16, :].reshape(TOKENS, BLOCK)
                    for part in range(3)
                ]
                hidden_t[2 * k + b] = act[0].T
                pairs[2 * k + b, :, 0:BLOCK] = act[1]
                pairs[2 * k + b, :, BLOCK:] = act[2]
            return carry

        lax.fori_loop(0, CHUNKS, relay, 0)

    first = step * GROUP
    gate_live = counts[0] - first
    down_live = counts[1] - first

    @pl.when(gate_live > 0)
    def _():
        for u in range(GROUP):
            spot = gate_slots[first + u]
            both = jnp.dot(x_t[spot // FPB], pairs[spot % FPB], preferred_element_type=F32)
            both = jnp.where(u < gate_live, both, 0.0).astype(BF16)
            gate_out[u] = both[:, 0:BLOCK]
            up_out[u] = both[:, BLOCK:]

    @pl.when(gate_live <= 0)
    def _():
        gate_out[...] = jnp.zeros_like(gate_out)
        up_out[...] = jnp.zeros_like(up_out)

    @pl.when(down_live > 0)
    def _():
        for u in range(GROUP):
            spot = down_slots[first + u]
            val = jnp.dot(hidden_t[spot % FPB], cots[spot // FPB], preferred_element_type=F32)
            down_out[u] = jnp.where(u < down_live, val, 0.0).astype(BF16)

    @pl.when(down_live <= 0)
    def _():
        down_out[...] = jnp.zeros_like(down_out)


def run_grads(gate_slots, down_slots, counts, acts, xs):
    scalars = pl.BlockSpec(memory_space=pltpu.SMEM)
    whole = pl.BlockSpec(memory_space=pltpu.VMEM)
    blocks = pl.BlockSpec((GROUP, BLOCK, BLOCK), lambda s: (s, 0, 0))
    grads = jax.ShapeDtypeStruct((NB, BLOCK, BLOCK), BF16)
    return pl.pallas_call(
        grads_kernel,
        grid=(NB // GROUP,),
        out_shape=(grads, grads, grads),
        in_specs=[scalars, scalars, scalars, whole, whole],
        out_specs=(blocks, blocks, blocks),
        scratch_shapes=[
            pltpu.VMEM((DPB, BLOCK, TOKENS), BF16),
            pltpu.VMEM((DPB, TOKENS, BLOCK), BF16),
            pltpu.VMEM((FPB, TOKENS, 2 * BLOCK), BF16),
            pltpu.VMEM((FPB, BLOCK, TOKENS), BF16),
        ],
        compiler_params=pltpu.CompilerParams(vmem_limit_bytes=40 * 2**20),
        name="block_grads",
    )(gate_slots, down_slots, counts, acts, xs)


def slot_of(slots, count):
    ids = jnp.arange(NB, dtype=jnp.int32)
    spots = jnp.arange(DPB * FPB, dtype=jnp.int32)
    hit = (slots[None, :] == spots[:, None]) & (ids < count)[None, :]
    return jnp.min(jnp.where(hit, ids[None, :], NB), axis=1)


def local(
    inputs,
    grad_out,
    gate_blocks,
    up_blocks,
    down_blocks,
    gate_slots,
    gate_count,
    down_slots,
    down_count,
):
    gate_slots, down_slots = gate_slots[0, 0], down_slots[0, 0]
    gate_count, down_count = gate_count[0, 0], down_count[0, 0]
    layer_out, grad_x, acts, xs = run_layer(
        slot_of(gate_slots, gate_count),
        slot_of(down_slots, down_count),
        inputs,
        grad_out,
        gate_blocks[0, 0],
        up_blocks[0, 0],
        down_blocks[0, 0],
    )
    counts = jnp.stack([gate_count, down_count])
    grads = run_grads(gate_slots, down_slots, counts, acts, xs)
    return (layer_out, grad_x) + tuple(grad[None, None] for grad in grads)


def solution(mesh):
    tokens = P("col", "row")
    blocks = P("row", "col", None, None, None)
    slots = P("row", "col", None)
    count = P("row", "col")
    return jax.shard_map(
        local,
        mesh=mesh,
        in_specs=(tokens, tokens, blocks, blocks, blocks, slots, count, slots, count),
        out_specs=(tokens, tokens, blocks, blocks, blocks),
        check_vma=False,
    )
```

profile of v0, /device:TPU:1, one launch (start us, length us, event | category | flops | bytes accessed | tf_op | source)
XLA Modules:
  0.0 142.6 jit_solution(7829884436701763805)
XLA Ops:
  1.9 0.1 pad_add_fusion.counts
  2.0 1.4 select_reduce_fusion
  3.4 0.0 copy-start.2
  3.4 0.0 copy-start.3
  3.4 123.0 %layer.1 = (bf16[32,1024]{1,0:T(8,128)(2,1)}, bf16[32,1024]{1,0:T(8,128)(2,1)}, bf16[13,4,4,2,48,128]{5,4,3,2,1,0:T(8,128)(2,1)}, bf16[8,2,32,1024]{3,2,1,0:T(8,128)(2,1)}) custom-call(s32[208]{0:T(256)} %get-tuple-element.20.gate_at, s32[208]{0:T(256)} %get-tuple-element.19.down_at, bf16[32,1024]{1,0:T(8,128)(2,1)} %x_in.1, bf16[32,1024]{1,0:T(8,128)(2,1)} %cot_in.1, ...), custom_call_target="tpu_custom_call" | custom-call | tf_op jit(solution)/shard_map/layer/pallas_call | solution.py:423
  126.4 0.0 copy-done.2
  126.4 0.0 copy-done.3
  126.4 0.0 copy-start
  126.4 2.4 %copy-done = bf16[13,4,4,2,48,128]{5,4,3,2,1,0:T(8,128)(2,1)S(1)} copy-done((bf16[13,4,4,2,48,128]{5,4,3,2,1,0:T(8,128)(2,1)S(1)}, bf16[13,4,4,2,48,128]{5,4,3,2,1,0:T(8,128)(2,1)}, u32[]{:S(2)}) %copy-start) | copy-done | bytes 5111832
  128.9 0.0 copy-start.1
  128.9 1.2 copy-done.1
  130.1 0.0 copy-start.5
  130.1 0.0 copy-start.4
  130.1 11.2 %block_grads.1 = (bf16[96,128,128]{2,1,0:T(8,128)(2,1)}, bf16[96,128,128]{2,1,0:T(8,128)(2,1)}, bf16[96,128,128]{2,1,0:T(8,128)(2,1)}) custom-call(s32[96]{0:T(128)S(1)} %bitcast.19, s32[96]{0:T(128)S(1)} %bitcast.17, s32[2]{0:T(128)S(1)} %pad_add_fusion.counts, bf16[13,4,4,2,48,128]{5,4,3,2,1,0:T(8,128)(2,1)S(1)} %copy-done, ...), custom_call_target="tpu_custom_call" | custom-call | tf_op jit(solution)/shard_map/block_grads/pallas_call | solution.py:536
  141.4 0.0 copy-done.5
  141.4 0.6 copy.18
  142.0 0.0 copy-done.4
  142.0 0.6 copy.19
  (2 shorter events, 0.0 us)
Async XLA Ops:
  3.4 123.0 %copy-start.2 = (s32[1,1,96]{2,1,0:T(1,128)S(1)}, s32[1,1,96]{2,1,0:T(1,128)}, u32[]{:S(2)}) copy-start(s32[1,1,96]{2,1,0:T(1,128)} %param.16) | copy-start | bytes 1156
  3.4 123.0 %copy-start.3 = (s32[1,1,96]{2,1,0:T(1,128)S(1)}, s32[1,1,96]{2,1,0:T(1,128)}, u32[]{:S(2)}) copy-start(s32[1,1,96]{2,1,0:T(1,128)} %param.14) | copy-start | bytes 1156
  126.4 2.5 %copy-start = (bf16[13,4,4,2,48,128]{5,4,3,2,1,0:T(8,128)(2,1)S(1)}, bf16[13,4,4,2,48,128]{5,4,3,2,1,0:T(8,128)(2,1)}, u32[]{:S(2)}) copy-start(bf16[13,4,4,2,48,128]{5,4,3,2,1,0:T(8,128)(2,1)} %get-tuple-element.14.acts) | copy-start | bytes 15335428
  128.9 1.2 copy-start.1
  130.1 11.2 %copy-start.5 = (bf16[32,1024]{1,0:T(8,128)(2,1)S(1)}, bf16[32,1024]{1,0:T(8,128)(2,1)}, u32[]{:S(2)}) copy-start(bf16[32,1024]{1,0:T(8,128)(2,1)} %get-tuple-element.26) | copy-start | bytes 196612
  130.1 11.9 %copy-start.4 = (bf16[32,1024]{1,0:T(8,128)(2,1)S(1)}, bf16[32,1024]{1,0:T(8,128)(2,1)}, u32[]{:S(2)}) copy-start(bf16[32,1024]{1,0:T(8,128)(2,1)} %get-tuple-element.27) | copy-start | bytes 196612
where the time goes:
time: 143 us
  Pallas kernels  134 us (94%)
  local copies, waits for them, and re-layouts  4.94 us (3%)
  between operations  1.97 us (1%)
  other arithmetic  1.46 us (1%)
    pallas_call x1, Pallas kernels, run_layer(): pl.pallas_call(layer_kernel, out_shape=(jax.ShapeDtypeStruct((32, WIDTH),...  123 us
    pallas_call x1, Pallas kernels, run_grads(): pl.pallas_call(grads_kernel, grid=(NB // GROUP,), out_shape=(grads, grads...  11.2 us
    unnamed x14, local copies, waits for them, and re-layouts  4.94 us

commit v1 on v0

v1 whole, which is shorter than its diff:
```python
import jax
import jax.numpy as jnp
from jax import lax
from jax.experimental import pallas as pl
from jax.experimental.pallas import tpu as pltpu
from jax.sharding import PartitionSpec as P

TOKENS = 256
BLOCK = 128
NB = 96
DPB = 8
FPB = 26
WIDTH = DPB * BLOCK
CHUNK = 2 * BLOCK
CHUNKS = FPB // 2
GROUP = 16
LAGS = (0, 4, 8, 12, 16, 20, 24, 28, 32)
MESH = pl.DeviceIdType.MESH
F32 = jnp.float32
BF16 = jnp.bfloat16


def nt_dot(a, b):
    return lax.dot_general(a, b, (((1,), (1,)), ((), ())), preferred_element_type=F32)


def layer_kernel(
    gate_at,
    down_at,
    x_in,
    cot_in,
    gate_in,
    up_in,
    down_in,
    layer_ref,
    hidden_out,
    pairs_out,
    x_out,
    cots_out,
    xs,
    raw_gate,
    raw_up,
    raw_down,
    w_gate,
    w_up,
    w_down,
    terms,
    half_al,
    half_ar,
    full_al,
    full_ar,
    sums,
    half_bl,
    half_br,
    full_bl,
    full_br,
    acts,
    hidden_t,
    pairs,
    x_t,
    cots,
    out_acc,
    gradx_acc,
    tail,
    tail_out,
    tail_core,
    tail_hl,
    tail_hr,
    tail_fl,
    tail_fr,
    load_sem,
    save_sem,
    head_send,
    head_recv,
    send_sem,
    recv_sem,
    tail_send,
    tail_recv,
):
    row, col = lax.axis_index("row"), lax.axis_index("col")
    z, y = row // 4, row % 4
    ix, core = col // 2, col % 2

    def y_dev(step):
        return (z * 4 + (y + step) % 4, col)

    def z_dev(step):
        return (((z + step) % 4) * 4 + y, col)

    def x_dev(step):
        return (row, ((ix + step) % 4) * 2 + core)

    sibling = (row, ix * 2 + 1 - core)

    loads = [
        pltpu.make_async_copy(x_in, xs.at[col, 0], load_sem.at[0]),
        pltpu.make_async_copy(cot_in, xs.at[col, 1], load_sem.at[1]),
        pltpu.make_async_copy(gate_in, raw_gate.at[pl.ds(0, NB)], load_sem.at[2]),
        pltpu.make_async_copy(up_in, raw_up.at[pl.ds(0, NB)], load_sem.at[3]),
        pltpu.make_async_copy(down_in, raw_down.at[pl.ds(0, NB)], load_sem.at[4]),
    ]
    for load in loads:
        load.start()

    barrier = pltpu.get_barrier_semaphore()
    for dev in (y_dev(1), y_dev(3), z_dev(1), z_dev(3), x_dev(1), x_dev(3), sibling):
        pl.semaphore_signal(barrier, inc=1, device_id=dev, device_id_type=MESH)

    zero = jnp.zeros((BLOCK, BLOCK), BF16)
    raw_gate[NB] = zero
    raw_up[NB] = zero
    raw_down[NB] = zero
    out_acc[...] = jnp.zeros_like(out_acc)
    gradx_acc[...] = jnp.zeros_like(gradx_acc)

    pl.semaphore_wait(barrier, 7)

    def head(n, src, dst, dev):
        return pltpu.make_async_remote_copy(
            src_ref=src,
            dst_ref=dst,
            send_sem=head_send.at[n],
            recv_sem=head_recv.at[n],
            device_id=dev,
            device_id_type=MESH,
        )

    other = 1 - core
    right, left = x_dev(1), x_dev(3)
    sent = []

    def at_x(step, side, arr):
        return xs.at[((ix + step) % 4) * 2 + side, arr]

    def head_start(n, src, dst, dev):
        one = head(n, src, dst, dev)
        one.start()
        sent.append(one)

    def forward(n, ref, dev):
        head_start(n, ref, ref, dev)

    def head_wait(n, ref):
        head(n, ref, ref, right).wait_recv()

    head_start(0, x_in, xs.at[col, 0], right)
    head_start(1, cot_in, xs.at[col, 1], left)
    head_start(2, cot_in, xs.at[col, 1], right)
    head_start(3, x_in, xs.at[col, 0], left)
    head_start(4, x_in, xs.at[col, 0], sibling)
    head_start(5, cot_in, xs.at[col, 1], sibling)

    def place_gate(k, carry):
        for raw, dense in ((raw_gate, w_gate), (raw_up, w_up)):
            for r in range(DPB):
                for b in range(2):
                    slot = gate_at[r * FPB + 2 * k + b]
                    dense[k, r * BLOCK : (r + 1) * BLOCK, b * BLOCK : (b + 1) * BLOCK] = raw[slot]
        return carry

    def place_down(k, carry):
        for r in range(DPB):
            for b in range(2):
                slot = down_at[r * FPB + 2 * k + b]
                w_down[k, b * BLOCK : (b + 1) * BLOCK, r * BLOCK : (r + 1) * BLOCK] = raw_down[slot]
        return carry

    loads[2].wait()
    loads[3].wait()
    lax.fori_loop(0, 4, place_gate, 0)

    head_wait(0, at_x(3, core, 0))
    forward(6, at_x(3, core, 0), right)
    forward(7, at_x(3, core, 0), sibling)
    head_wait(1, at_x(1, core, 1))
    forward(8, at_x(1, core, 1), left)
    forward(9, at_x(1, core, 1), sibling)

    lax.fori_loop(4, 8, place_gate, 0)

    head_wait(2, at_x(3, core, 1))
    forward(10, at_x(3, core, 1), sibling)
    head_wait(3, at_x(1, core, 0))
    forward(11, at_x(1, core, 0), sibling)

    lax.fori_loop(8, CHUNKS, place_gate, 0)
    loads[4].wait()
    lax.fori_loop(0, 4, place_down, 0)

    head_wait(6, at_x(2, core, 0))
    forward(12, at_x(2, core, 0), sibling)
    head_wait(8, at_x(2, core, 1))
    forward(13, at_x(2, core, 1), sibling)

    lax.fori_loop(4, CHUNKS, place_down, 0)

    head_wait(4, at_x(0, other, 0))
    head_wait(5, at_x(0, other, 1))
    head_wait(7, at_x(3, other, 0))
    head_wait(9, at_x(1, other, 1))
    head_wait(10, at_x(3, other, 1))
    head_wait(11, at_x(1, other, 0))
    head_wait(12, at_x(2, other, 0))
    head_wait(13, at_x(2, other, 1))
    loads[0].wait()
    loads[1].wait()

    save_x = pltpu.make_async_copy(x_t, x_out, save_sem.at[2 * CHUNKS])
    save_cots = pltpu.make_async_copy(cots, cots_out, save_sem.at[2 * CHUNKS + 1])

    def lay_out_inputs():
        for r in range(DPB):
            cols = slice(r * BLOCK, (r + 1) * BLOCK)
            x_t[r] = xs[:, 0, :, cols].reshape(TOKENS, BLOCK).T
            cots[r] = xs[:, 1, :, cols].reshape(TOKENS, BLOCK)
        save_x.start()
        save_cots.start()

    def places(k):
        odd = k % 2
        i = (1 - odd) * y + odd * z
        j = (1 - odd) * z + odd * y

        def dev(step, along_z):
            y_new = (y + (1 - along_z) * step) % 4
            z_new = (z + along_z * step) % 4
            return (z_new * 4 + y_new, col)

        return i, j, dev(1, odd), dev(3, odd), dev(1, 1 - odd), dev(3, 1 - odd)

    def copy(k, n, src, dst, dev):
        return pltpu.make_async_remote_copy(
            src_ref=src,
            dst_ref=dst,
            send_sem=send_sem.at[k, n],
            recv_sem=recv_sem.at[k, n],
            device_id=dev,
            device_id_type=MESH,
        )

    def all_copies(k):
        i, j, ar, al, br, bl = places(k)
        i1, i2, i3 = (i + 1) % 4, (i + 2) % 4, (i + 3) % 4
        j1, j2, j3 = (j + 1) % 4, (j + 2) % 4, (j + 3) % 4
        same = lambda n, ref, dev: copy(k, n, ref, ref, dev)
        near, far = pl.ds(0, 2), pl.ds(2, 2)
        return [
            lambda: copy(k, 0, terms.at[k, i2, 0], half_al.at[k], ar),
            lambda: copy(k, 1, terms.at[k, i2, 1], half_ar.at[k], al),
            lambda: copy(k, 2, terms.at[k, i1, 1], full_al.at[k, 1], ar),
            lambda: copy(k, 3, terms.at[k, i3, 0], full_ar.at[k, 0], al),
            lambda: copy(k, 4, terms.at[k, i1, 0], full_al.at[k, 0], ar),
            lambda: copy(k, 5, terms.at[k, i3, 1], full_ar.at[k, 1], al),
            lambda: copy(k, 6, sums.at[k, j2, 0], half_bl.at[k], br),
            lambda: copy(k, 7, sums.at[k, j2, 1], half_br.at[k], bl),
            lambda: copy(k, 8, sums.at[k, j1], full_bl.at[k], br),
            lambda: copy(k, 9, sums.at[k, j3], full_br.at[k], bl),
            lambda: same(10, acts.at[k, i, j], br),
            lambda: same(11, acts.at[k, i, j], bl),
            lambda: same(12, acts.at[k, i, j3, 0], br),
            lambda: same(13, acts.at[k, i, j1, 1], bl),
            lambda: same(14, acts.at[k, i, near], ar),
            lambda: same(15, acts.at[k, i, far], al),
            lambda: same(16, acts.at[k, i, far], ar),
            lambda: same(17, acts.at[k, i, near], al),
            lambda: same(18, acts.at[k, i3, near], ar),
            lambda: same(19, acts.at[k, i1, far], al),
        ]

    def arrived(k, n, ref):
        i, j, ar, al, br, bl = places(k)
        copy(k, n, ref, ref, ar).wait_recv()

    def plus(a, b):
        return (a.astype(F32) + b.astype(F32)).astype(BF16)

    def p0(k):
        for part, (arr, weights) in enumerate(((0, w_gate), (0, w_up), (1, w_down))):
            if part < 2:
                lhs = xs[:, 0].reshape(TOKENS, WIDTH)
                val = jnp.dot(lhs, weights[k], preferred_element_type=F32)
            else:
                lhs = xs[:, 1].reshape(TOKENS, WIDTH)
                val = nt_dot(lhs, weights[k])
            val = val.astype(BF16)
            for b in range(2):
                terms[k, :, b, :, part * 16 : (part + 1) * 16, :] = val[
                    :, b * BLOCK : (b + 1) * BLOCK
                ].reshape(4, 4, 16, BLOCK)
        copies = all_copies(k)
        for n in range(4):
            copies[n]().start()

    def p1(k):
        i, j, *_ = places(k)
        i1, i3 = (i + 1) % 4, (i + 3) % 4
        copies = all_copies(k)
        arrived(k, 0, half_al.at[k])
        terms[k, i1, 0] = plus(terms[k, i1, 0], half_al[k])
        copies[4]().start()
        arrived(k, 1, half_ar.at[k])
        terms[k, i3, 1] = plus(terms[k, i3, 1], half_ar[k])
        copies[5]().start()

    def p2(k):
        i, j, *_ = places(k)
        copies = all_copies(k)
        arrived(k, 2, full_al.at[k, 1])
        arrived(k, 3, full_ar.at[k, 0])
        arrived(k, 4, full_al.at[k, 0])
        arrived(k, 5, full_ar.at[k, 1])
        for b in range(2):
            total = terms[k, i, b].astype(F32) + full_al[k, b].astype(F32)
            sums[k, :, b] = (total + full_ar[k, b].astype(F32)).astype(BF16)
        copies[6]().start()
        copies[7]().start()

    def p3(k):
        i, j, *_ = places(k)
        j1, j3 = (j + 1) % 4, (j + 3) % 4
        copies = all_copies(k)
        arrived(k, 6, half_bl.at[k])
        sums[k, j1, 0] = plus(sums[k, j1, 0], half_bl[k])
        copies[8]().start()
        arrived(k, 7, half_br.at[k])
        sums[k, j3, 1] = plus(sums[k, j3, 1], half_br[k])
        copies[9]().start()

    def p4(k):
        i, j, *_ = places(k)
        copies = all_copies(k)
        arrived(k, 8, full_bl.at[k])
        arrived(k, 9, full_br.at[k])
        total = sums[k, j].astype(F32) + full_bl[k].astype(F32) + full_br[k].astype(F32)
        gate, up, grad = total[:, 0:16], total[:, 16:32], total[:, 32:48]
        sigma = 1.0 / (1.0 + jnp.exp(-gate))
        acts[k, i, j, :, 0:16, :] = (gate * sigma * up).astype(BF16)
        acts[k, i, j, :, 16:32, :] = (grad * up * sigma * (1.0 + gate * (1.0 - sigma))).astype(BF16)
        acts[k, i, j, :, 32:48, :] = (grad * gate * sigma).astype(BF16)
        copies[10]().start()
        copies[11]().start()

    def p5(k):
        i, j, *_ = places(k)
        copies = all_copies(k)
        arrived(k, 10, acts.at[k, i, (j + 3) % 4])
        copies[12]().start()
        arrived(k, 11, acts.at[k, i, (j + 1) % 4])
        copies[13]().start()

    def p6(k):
        i, j, *_ = places(k)
        copies = all_copies(k)
        arrived(k, 12, acts.at[k, i, (j + 2) % 4, 0])
        arrived(k, 13, acts.at[k, i, (j + 2) % 4, 1])
        for n in range(14, 18):
            copies[n]().start()

    def p7(k):
        i, j, *_ = places(k)
        copies = all_copies(k)
        arrived(k, 14, acts.at[k, (i + 3) % 4, pl.ds(0, 2)])
        copies[18]().start()
        arrived(k, 15, acts.at[k, (i + 1) % 4, pl.ds(2, 2)])
        copies[19]().start()

    def saves(k):
        return (
            pltpu.make_async_copy(hidden_t.at[k], hidden_out.at[k], save_sem.at[2 * k]),
            pltpu.make_async_copy(pairs.at[k], pairs_out.at[k], save_sem.at[2 * k + 1]),
        )

    def p8(k):
        i, j, *_ = places(k)
        arrived(k, 16, acts.at[k, (i + 3) % 4, pl.ds(2, 2)])
        arrived(k, 17, acts.at[k, (i + 1) % 4, pl.ds(0, 2)])
        arrived(k, 18, acts.at[k, (i + 2) % 4, pl.ds(0, 2)])
        arrived(k, 19, acts.at[k, (i + 2) % 4, pl.ds(2, 2)])

        def act(part):
            cols = [
                acts[k, :, :, b, part * 16 : (part + 1) * 16, :].reshape(TOKENS, BLOCK)
                for b in range(2)
            ]
            return cols, jnp.concatenate(cols, axis=1)

        (_, hidden), (gate_cols, grad_gate), (up_cols, grad_up) = act(0), act(1), act(2)
        for n in range(4):
            cols = slice(n * 256, (n + 1) * 256)
            out = jnp.dot(hidden, w_down[k, :, cols], preferred_element_type=F32)
            out_acc[:, :, cols] += out.reshape(8, 32, 256)
            grad = nt_dot(grad_gate, w_gate[k, cols, :]) + nt_dot(grad_up, w_up[k, cols, :])
            gradx_acc[:, :, cols] += grad.reshape(8, 32, 256)
        hidden_t[k] = hidden.T
        for b in range(2):
            pairs[k, b, :, 0:BLOCK] = gate_cols[b]
            pairs[k, b, :, BLOCK:] = up_cols[b]
        for save in saves(k):
            save.start()
        for one in all_copies(k):
            one().wait_send()

    def tick(t, carry):
        for phase, late in zip((p7, p6, p5, p4, p3, p2, p1, p0, p8), LAGS[7::-1] + LAGS[8:]):
            k = t - late

            @pl.when(jnp.logical_and(k >= 0, k < CHUNKS))
            def _():
                phase(k)

        @pl.when(t == 6)
        def _():
            lay_out_inputs()

        return carry

    lax.fori_loop(0, CHUNKS + LAGS[8], tick, 0)

    def last(n, src, dst, dev):
        return pltpu.make_async_remote_copy(
            src_ref=src,
            dst_ref=dst,
            send_sem=tail_send.at[n],
            recv_sem=tail_recv.at[n],
            device_id=dev,
            device_id_type=MESH,
        )

    x0, x1, x2, x3 = ix, (ix + 1) % 4, (ix + 2) % 4, (ix + 3) % 4
    totals = (out_acc, gradx_acc)
    cores = {}
    for n, at in ((0, x2), (1, x1), (2, x3), (3, x0)):
        for arr in range(2):
            tail_out[at, arr] = totals[arr][at * 2 + other].astype(BF16)
        cores[n] = last(n, tail_out.at[at], tail_core.at[at], sibling)
        cores[n].start()

    def both(n, at):
        cores[n].wait_recv()
        for arr in range(2):
            mine = totals[arr][at * 2 + core] + tail_core[at, arr].astype(F32)
            tail[at, arr] = mine.astype(BF16)

    steps = [
        last(4, tail.at[x2, 0], tail_hl, right),
        last(5, tail.at[x2, 1], tail_hr, left),
        last(6, tail.at[x1, 1], tail_fl.at[1], right),
        last(7, tail.at[x3, 0], tail_fr.at[0], left),
        last(8, tail.at[x1, 0], tail_fl.at[0], right),
        last(9, tail.at[x3, 1], tail_fr.at[1], left),
    ]
    both(0, x2)
    steps[0].start()
    steps[1].start()
    both(1, x1)
    steps[2].start()
    both(2, x3)
    steps[3].start()
    steps[0].wait_recv()
    tail[x1, 0] = plus(tail[x1, 0], tail_hl[...])
    steps[4].start()
    steps[1].wait_recv()
    tail[x3, 1] = plus(tail[x3, 1], tail_hr[...])
    steps[5].start()
    cores[3].wait_recv()
    for n in (2, 3, 4, 5):
        steps[n].wait_recv()
    for arr in range(2):
        total = totals[arr][x0 * 2 + core] + tail_core[x0, arr].astype(F32)
        total = total + tail_fl[arr].astype(F32) + tail_fr[arr].astype(F32)
        layer_ref[arr] = total.astype(BF16)

    for one in sent + list(cores.values()) + steps:
        one.wait_send()
    save_x.wait()
    save_cots.wait()

    def saved(k, carry):
        for save in saves(k):
            save.wait()
        return carry

    lax.fori_loop(0, CHUNKS, saved, 0)


def run_layer(gate_at, down_at, inputs, grad_out, gate_blocks, up_blocks, down_blocks):
    anywhere = pl.BlockSpec(memory_space=pl.ANY)
    scalars = pl.BlockSpec(memory_space=pltpu.SMEM)
    vmem = pl.BlockSpec(memory_space=pltpu.VMEM)
    raw = pltpu.VMEM((NB + 1, BLOCK, BLOCK), BF16)
    part = (48, BLOCK)
    return pl.pallas_call(
        layer_kernel,
        out_shape=(
            jax.ShapeDtypeStruct((2, 32, WIDTH), BF16),
            jax.ShapeDtypeStruct((CHUNKS, CHUNK, TOKENS), BF16),
            jax.ShapeDtypeStruct((CHUNKS, 2, TOKENS, 2 * BLOCK), BF16),
            jax.ShapeDtypeStruct((DPB, BLOCK, TOKENS), BF16),
            jax.ShapeDtypeStruct((DPB, TOKENS, BLOCK), BF16),
        ),
        in_specs=[scalars, scalars] + [anywhere] * 5,
        out_specs=(vmem, anywhere, anywhere, anywhere, anywhere),
        scratch_shapes=[
            pltpu.VMEM((8, 2, 32, WIDTH), BF16),
            raw,
            raw,
            raw,
            pltpu.VMEM((CHUNKS, WIDTH, CHUNK), BF16),
            pltpu.VMEM((CHUNKS, WIDTH, CHUNK), BF16),
            pltpu.VMEM((CHUNKS, CHUNK, WIDTH), BF16),
            pltpu.VMEM((CHUNKS, 4, 2, 4) + part, BF16),
            pltpu.VMEM((CHUNKS, 4) + part, BF16),
            pltpu.VMEM((CHUNKS, 4) + part, BF16),
            pltpu.VMEM((CHUNKS, 2, 4) + part, BF16),
            pltpu.VMEM((CHUNKS, 2, 4) + part, BF16),
            pltpu.VMEM((CHUNKS, 4, 2) + part, BF16),
            pltpu.VMEM((CHUNKS,) + part, BF16),
            pltpu.VMEM((CHUNKS,) + part, BF16),
            pltpu.VMEM((CHUNKS, 2) + part, BF16),
            pltpu.VMEM((CHUNKS, 2) + part, BF16),
            pltpu.VMEM((CHUNKS, 4, 4, 2) + part, BF16),
            pltpu.VMEM((CHUNKS, CHUNK, TOKENS), BF16),
            pltpu.VMEM((CHUNKS, 2, TOKENS, 2 * BLOCK), BF16),
            pltpu.VMEM((DPB, BLOCK, TOKENS), BF16),
            pltpu.VMEM((DPB, TOKENS, BLOCK), BF16),
            pltpu.VMEM((8, 32, WIDTH), F32),
            pltpu.VMEM((8, 32, WIDTH), F32),
            pltpu.VMEM((4, 2, 32, WIDTH), BF16),
            pltpu.VMEM((4, 2, 32, WIDTH), BF16),
            pltpu.VMEM((4, 2, 32, WIDTH), BF16),
            pltpu.VMEM((32, WIDTH), BF16),
            pltpu.VMEM((32, WIDTH), BF16),
            pltpu.VMEM((2, 32, WIDTH), BF16),
            pltpu.VMEM((2, 32, WIDTH), BF16),
            pltpu.SemaphoreType.DMA((5,)),
            pltpu.SemaphoreType.DMA((2 * CHUNKS + 2,)),
            pltpu.SemaphoreType.DMA((14,)),
            pltpu.SemaphoreType.DMA((14,)),
            pltpu.SemaphoreType.DMA((CHUNKS, 20)),
            pltpu.SemaphoreType.DMA((CHUNKS, 20)),
            pltpu.SemaphoreType.DMA((10,)),
            pltpu.SemaphoreType.DMA((10,)),
        ],
        compiler_params=pltpu.CompilerParams(
            collective_id=0, has_side_effects=True, vmem_limit_bytes=60 * 2**20
        ),
        name="layer",
    )(gate_at, down_at, inputs, grad_out, gate_blocks, up_blocks, down_blocks)


def grads_kernel(
    gate_slots,
    down_slots,
    counts,
    layer_in,
    hidden_in,
    pairs_in,
    x_in,
    cots_in,
    out_ref,
    gradx_ref,
    gate_out,
    up_out,
    down_out,
    hidden_t,
    pairs,
    x_t,
    cots,
    gate_stage,
    up_stage,
    down_stage,
    load_sem,
    save_sem,
):
    loads = [
        pltpu.make_async_copy(cots_in, cots, load_sem.at[0]),
        pltpu.make_async_copy(hidden_in, hidden_t, load_sem.at[1]),
        pltpu.make_async_copy(x_in, x_t, load_sem.at[2]),
        pltpu.make_async_copy(pairs_in, pairs, load_sem.at[3]),
    ]
    for load in loads:
        load.start()
    out_ref[...] = layer_in[0]
    gradx_ref[...] = layer_in[1]
    groups = NB // GROUP

    def save(kind, stage, out, g):
        rows = pl.ds(g * GROUP, GROUP)
        return pltpu.make_async_copy(stage.at[rows], out.at[rows], save_sem.at[kind, g])

    loads[0].wait()
    loads[1].wait()

    def down_group(g, carry):
        first = g * GROUP
        live = counts[1] - first

        @pl.when(live > 0)
        def _():
            for u in range(GROUP):
                spot = down_slots[first + u]
                val = jnp.dot(hidden_t[spot % FPB], cots[spot // FPB], preferred_element_type=F32)
                down_stage[first + u] = jnp.where(u < live, val, 0.0).astype(BF16)

        @pl.when(live <= 0)
        def _():
            down_stage[pl.ds(first, GROUP)] = jnp.zeros((GROUP, BLOCK, BLOCK), BF16)

        save(0, down_stage, down_out, g).start()
        return carry

    lax.fori_loop(0, groups, down_group, 0)
    loads[2].wait()
    loads[3].wait()

    def gate_group(g, carry):
        first = g * GROUP
        live = counts[0] - first

        @pl.when(live > 0)
        def _():
            for u in range(GROUP):
                spot = gate_slots[first + u]
                val = jnp.dot(x_t[spot // FPB], pairs[spot % FPB], preferred_element_type=F32)
                val = jnp.where(u < live, val, 0.0).astype(BF16)
                gate_stage[first + u] = val[:, 0:BLOCK]
                up_stage[first + u] = val[:, BLOCK:]

        @pl.when(live <= 0)
        def _():
            zero = jnp.zeros((GROUP, BLOCK, BLOCK), BF16)
            gate_stage[pl.ds(first, GROUP)] = zero
            up_stage[pl.ds(first, GROUP)] = zero

        save(1, gate_stage, gate_out, g).start()
        save(2, up_stage, up_out, g).start()
        return carry

    lax.fori_loop(0, groups, gate_group, 0)

    def finish(g, carry):
        save(0, down_stage, down_out, g).wait()
        save(1, gate_stage, gate_out, g).wait()
        save(2, up_stage, up_out, g).wait()
        return carry

    lax.fori_loop(0, groups, finish, 0)


def run_grads(gate_slots, down_slots, counts, layer, hidden, pairs, x_t, cots):
    scalars = pl.BlockSpec(memory_space=pltpu.SMEM)
    vmem = pl.BlockSpec(memory_space=pltpu.VMEM)
    anywhere = pl.BlockSpec(memory_space=pl.ANY)
    grads = jax.ShapeDtypeStruct((NB, BLOCK, BLOCK), BF16)
    tokens = jax.ShapeDtypeStruct((32, WIDTH), BF16)
    return pl.pallas_call(
        grads_kernel,
        out_shape=(tokens, tokens, grads, grads, grads),
        in_specs=[scalars, scalars, scalars, vmem] + [anywhere] * 4,
        out_specs=(vmem, vmem, anywhere, anywhere, anywhere),
        scratch_shapes=[
            pltpu.VMEM((FPB, BLOCK, TOKENS), BF16),
            pltpu.VMEM((FPB, TOKENS, 2 * BLOCK), BF16),
            pltpu.VMEM((DPB, BLOCK, TOKENS), BF16),
            pltpu.VMEM((DPB, TOKENS, BLOCK), BF16),
            pltpu.VMEM((NB, BLOCK, BLOCK), BF16),
            pltpu.VMEM((NB, BLOCK, BLOCK), BF16),
            pltpu.VMEM((NB, BLOCK, BLOCK), BF16),
            pltpu.SemaphoreType.DMA((4,)),
            pltpu.SemaphoreType.DMA((3, NB // GROUP)),
        ],
        compiler_params=pltpu.CompilerParams(vmem_limit_bytes=60 * 2**20),
        name="block_grads",
    )(gate_slots, down_slots, counts, layer, hidden, pairs, x_t, cots)


def slot_of(slots, count):
    ids = jnp.arange(NB, dtype=jnp.int32)
    spots = jnp.arange(DPB * FPB, dtype=jnp.int32)
    hit = (slots[None, :] == spots[:, None]) & (ids < count)[None, :]
    return jnp.min(jnp.where(hit, ids[None, :], NB), axis=1)


def local(
    inputs,
    grad_out,
    gate_blocks,
    up_blocks,
    down_blocks,
    gate_slots,
    gate_count,
    down_slots,
    down_count,
):
    gate_slots, down_slots = gate_slots[0, 0], down_slots[0, 0]
    gate_count, down_count = gate_count[0, 0], down_count[0, 0]
    layer, hidden, pairs, x_t, cots = run_layer(
        slot_of(gate_slots, gate_count),
        slot_of(down_slots, down_count),
        inputs,
        grad_out,
        gate_blocks[0, 0],
        up_blocks[0, 0],
        down_blocks[0, 0],
    )
    counts = jnp.stack([gate_count, down_count])
    hidden = hidden.reshape(FPB, BLOCK, TOKENS)
    pairs = pairs.reshape(FPB, TOKENS, 2 * BLOCK)
    layer_out, grad_x, *grads = run_grads(
        gate_slots, down_slots, counts, layer, hidden, pairs, x_t, cots
    )
    return (layer_out, grad_x) + tuple(grad[None, None] for grad in grads)


def solution(mesh):
    tokens = P("col", "row")
    blocks = P("row", "col", None, None, None)
    slots = P("row", "col", None)
    count = P("row", "col")
    return jax.shard_map(
        local,
        mesh=mesh,
        in_specs=(tokens, tokens, blocks, blocks, blocks, slots, count, slots, count),
        out_specs=(tokens, tokens, blocks, blocks, blocks),
        check_vma=False,
    )
```

time: 143 us -> 103 us (0.72)
  Pallas kernels: 134 us -> 98.1 us
  local copies, waits for them, and re-layouts: 4.94 us -> 0 us
    pallas_call x2, Pallas kernels: 134 us -> 98.1 us  [the longest x1 90.5 us: run_layer(): pl.pallas_call(layer_kernel, out_shape=(jax.ShapeDtypeStruct((2, 32, WIDT...]
    unnamed x14 -> x0, local copies, waits for them, and re-layouts: 4.94 us -> none
where the time goes in v1:
time: 103 us; the launch traced here: 102 us
  Pallas kernels  98.1 us (95%)
  other arithmetic  1.97 us (2%)
  between operations  1.93 us (2%)
    pallas_call x1, Pallas kernels, run_layer(): pl.pallas_call(layer_kernel, out_shape=(jax.ShapeDtypeStruct((2, 32, WIDT...  90.5 us
    pallas_call x1, Pallas kernels, run_grads(): pl.pallas_call(grads_kernel, out_shape=(tokens, tokens, grads, grads, gra...  7.58 us

profile of v1, /device:TPU:1, one launch (start us, length us, event | category | flops | bytes accessed | tf_op | source)
XLA Modules:
  0.0 102.0 jit_solution(4073935740318264059)
XLA Ops:
  1.9 0.6 pad_add_fusion.counts
  2.5 1.4 %select_reduce_fusion = (s32[208]{0:T(256)}, s32[208]{0:T(256)}) fusion(s32[96]{0:T(128)} %bitcast.25, pred[96]{0:T(512)(128)(4,1)S(1)} %iota_compare_fusion.2, pred[96]{0:T(512)(128)(4,1)S(1)} %iota_compare_fusion.3, s32[96]{0:T(128)} %bitcast.23), kind=kLoop, calls=%fused_computation | loop fusion | flops 159328 | bytes 2624 | tf_op jit(solution)/shard_map/reduce_min | solution.py:681
  3.9 90.5 %layer.1 = (bf16[2,32,1024]{2,1,0:T(8,128)(2,1)}, bf16[13,256,256]{2,1,0:T(8,128)(2,1)}, bf16[13,2,256,256]{3,2,1,0:T(8,128)(2,1)}, bf16[8,128,256]{2,1,0:T(8,128)(2,1)}, bf16[8,256,128]{2,1,0:T(8,128)(2,1)}) custom-call(s32[208]{0:T(256)} %get-tuple-element.26.gate_at, s32[208]{0:T(256)} %get-tuple-element.25.down_at, bf16[32,1024]{1,0:T(8,128)(2,1)} %x_in.1, ...), custom_call_target="tpu_custom_call" | custom-call | tf_op jit(solution)/shard_map/layer/pallas_call | solution.py:492
  94.4 7.6 %block_grads.1 = (bf16[32,1024]{1,0:T(8,128)(2,1)}, bf16[32,1024]{1,0:T(8,128)(2,1)}, bf16[96,128,128]{2,1,0:T(8,128)(2,1)}, bf16[96,128,128]{2,1,0:T(8,128)(2,1)}, bf16[96,128,128]{2,1,0:T(8,128)(2,1)}) custom-call(s32[96]{0:T(128)} %bitcast.24, s32[96]{0:T(128)} %bitcast.26, s32[2]{0:T(128)} %pad_add_fusion.counts, ...), custom_call_target="tpu_custom_call" | custom-call | tf_op jit(solution)/shard_map/block_grads/pallas_call | solution.py:656
  (2 shorter events, 0.0 us)

commit v2 on v1

v2 whole, which is shorter than its diff:
```python
import jax
import jax.numpy as jnp
from jax import lax
from jax.experimental import pallas as pl
from jax.experimental.pallas import tpu as pltpu
from jax.sharding import PartitionSpec as P

TOKENS = 256
BLOCK = 128
NB = 96
DPB = 8
FPB = 26
WIDTH = DPB * BLOCK
CHUNK = 2 * BLOCK
CHUNKS = FPB // 2
GROUP = 16
LAGS = (0, 4, 8, 12, 16, 20, 24, 28, 32)
MESH = pl.DeviceIdType.MESH
HEAD_SEM = (0, 1, 2, 3, 6, 6, 4, 6, 5, 6, 6, 6, 6, 6)
SEND_SEM = (0,) * 6 + (1,) * 8 + (2,) * 6
RECV_SEM = (0, 0, 1, 1, 1, 1, 2, 2, 3, 3, 4, 4, 5, 5, 6, 6, 7, 7, 7, 7)
F32 = jnp.float32
BF16 = jnp.bfloat16


def nt_dot(a, b):
    return lax.dot_general(a, b, (((1,), (1,)), ((), ())), preferred_element_type=F32)


def layer_kernel(
    gate_slots,
    gate_count,
    down_slots,
    down_count,
    x_in,
    cot_in,
    gate_in,
    up_in,
    down_in,
    part1_ref,
    part2_ref,
    part3_ref,
    mine_ref,
    hidden_out,
    pairs_out,
    x_out,
    cots_out,
    xs,
    raw_gate,
    raw_up,
    raw_down,
    w_gate,
    w_up,
    w_down,
    terms,
    half_a,
    full_a,
    sums,
    half_b,
    full_b,
    acts,
    hidden_t,
    pairs,
    x_t,
    cots,
    out_acc,
    gradx_acc,
    tail_out,
    tail_core,
    tables,
    slot_at,
    load_sem,
    save_sem,
    head_send,
    head_recv,
    send_sem,
    recv_sem,
    tail_send,
    tail_recv,
):
    row, col = lax.axis_index("row"), lax.axis_index("col")
    z, y = row // 4, row % 4
    ix, core = col // 2, col % 2

    def y_dev(step):
        return (z * 4 + (y + step) % 4, col)

    def z_dev(step):
        return (((z + step) % 4) * 4 + y, col)

    def x_dev(step):
        return (row, ((ix + step) % 4) * 2 + core)

    sibling = (row, ix * 2 + 1 - core)

    loads = [
        pltpu.make_async_copy(x_in, xs.at[col, 0], load_sem.at[0]),
        pltpu.make_async_copy(cot_in, xs.at[col, 1], load_sem.at[1]),
        pltpu.make_async_copy(gate_in, raw_gate.at[pl.ds(0, NB)], load_sem.at[2]),
        pltpu.make_async_copy(up_in, raw_up.at[pl.ds(0, NB)], load_sem.at[3]),
        pltpu.make_async_copy(down_in, raw_down.at[pl.ds(0, NB)], load_sem.at[4]),
    ]
    loads[0].start()
    loads[1].start()

    barrier = pltpu.get_barrier_semaphore()
    for dev in (y_dev(1), y_dev(3), z_dev(1), z_dev(3), x_dev(1), x_dev(3), sibling):
        pl.semaphore_signal(barrier, inc=1, device_id=dev, device_id_type=MESH)

    zero = jnp.zeros((BLOCK, BLOCK), BF16)
    raw_gate[NB] = zero
    raw_up[NB] = zero
    raw_down[NB] = zero
    out_acc[...] = jnp.zeros_like(out_acc)
    gradx_acc[...] = jnp.zeros_like(gradx_acc)

    pl.semaphore_wait(barrier, 7)

    def head(n, src, dst, dev):
        return pltpu.make_async_remote_copy(
            src_ref=src,
            dst_ref=dst,
            send_sem=head_send.at[0],
            recv_sem=head_recv.at[HEAD_SEM[n]],
            device_id=dev,
            device_id_type=MESH,
        )

    other = 1 - core
    right, left = x_dev(1), x_dev(3)

    def at_x(step, side, arr):
        return xs.at[((ix + step) % 4) * 2 + side, arr]

    def head_start(n, src, dst, dev):
        head(n, src, dst, dev).start()

    def forward(n, ref, dev):
        head_start(n, ref, ref, dev)

    def head_wait(n, ref):
        head(n, ref, ref, right).wait_recv()

    head_start(0, x_in, xs.at[col, 0], right)
    head_start(1, cot_in, xs.at[col, 1], left)
    head_start(2, cot_in, xs.at[col, 1], right)
    head_start(3, x_in, xs.at[col, 0], left)
    head_start(4, x_in, xs.at[col, 0], sibling)
    head_start(5, cot_in, xs.at[col, 1], sibling)
    for load in loads[2:]:
        load.start()

    spots = lax.broadcasted_iota(jnp.int32, (8, 128), 0) * 128 + lax.broadcasted_iota(
        jnp.int32, (8, 128), 1
    )

    def enter(n, both):
        gate_tab, down_tab = both
        gate_tab = jnp.where(spots == gate_slots[0, 0, n], n, gate_tab)
        down_tab = jnp.where(spots == down_slots[0, 0, n], n, down_tab)
        return gate_tab, down_tab

    nowhere = jnp.full((8, 128), NB, jnp.int32)
    gate_tab, down_tab = lax.fori_loop(0, NB, enter, (nowhere, nowhere), unroll=8)
    tables[0] = jnp.where(gate_tab < gate_count[0, 0], gate_tab, NB)
    tables[1] = jnp.where(down_tab < down_count[0, 0], down_tab, NB)
    to_scalars = pltpu.make_async_copy(tables, slot_at, load_sem.at[5])
    to_scalars.start()

    def find(table, spot):
        return slot_at[table, spot // 128, spot % 128]

    def place_gate(k, carry):
        for raw, dense in ((raw_gate, w_gate), (raw_up, w_up)):
            for r in range(DPB):
                for b in range(2):
                    slot = find(0, r * FPB + 2 * k + b)
                    dense[k, r * BLOCK : (r + 1) * BLOCK, b * BLOCK : (b + 1) * BLOCK] = raw[slot]
        return carry

    def place_down(k, carry):
        for r in range(DPB):
            for b in range(2):
                slot = find(1, r * FPB + 2 * k + b)
                w_down[k, b * BLOCK : (b + 1) * BLOCK, r * BLOCK : (r + 1) * BLOCK] = raw_down[slot]
        return carry

    to_scalars.wait()
    loads[2].wait()
    loads[3].wait()
    lax.fori_loop(0, 4, place_gate, 0)

    head_wait(0, at_x(3, core, 0))
    forward(6, at_x(3, core, 0), right)
    forward(7, at_x(3, core, 0), sibling)
    head_wait(1, at_x(1, core, 1))
    forward(8, at_x(1, core, 1), left)
    forward(9, at_x(1, core, 1), sibling)

    lax.fori_loop(4, 8, place_gate, 0)

    head_wait(2, at_x(3, core, 1))
    forward(10, at_x(3, core, 1), sibling)
    head_wait(3, at_x(1, core, 0))
    forward(11, at_x(1, core, 0), sibling)

    lax.fori_loop(8, CHUNKS, place_gate, 0)
    loads[4].wait()
    lax.fori_loop(0, 4, place_down, 0)

    head_wait(6, at_x(2, core, 0))
    forward(12, at_x(2, core, 0), sibling)
    head_wait(8, at_x(2, core, 1))
    forward(13, at_x(2, core, 1), sibling)

    lax.fori_loop(4, CHUNKS, place_down, 0)

    head_wait(4, xs.at[pl.ds(0, 4)])
    loads[0].wait()
    loads[1].wait()

    save_x = pltpu.make_async_copy(x_t, x_out, save_sem.at[0])
    save_cots = pltpu.make_async_copy(cots, cots_out, save_sem.at[1])

    def lay_out_inputs():
        for r in range(DPB):
            cols = slice(r * BLOCK, (r + 1) * BLOCK)
            x_t[r] = xs[:, 0, :, cols].reshape(TOKENS, BLOCK).T
            cots[r] = xs[:, 1, :, cols].reshape(TOKENS, BLOCK)
        save_x.start()
        save_cots.start()

    def places(k):
        odd = k % 2
        i = (1 - odd) * y + odd * z
        j = (1 - odd) * z + odd * y

        def dev(step, along_z):
            y_new = (y + (1 - along_z) * step) % 4
            z_new = (z + along_z * step) % 4
            return (z_new * 4 + y_new, col)

        return i, j, dev(1, odd), dev(3, odd), dev(1, 1 - odd), dev(3, 1 - odd)

    def swap(k, a, b):
        turned = k // (CHUNKS - 1)
        return (1 - turned) * a + turned * b, (1 - turned) * b + turned * a

    def gather_places(k):
        i, j, ar, al, br, bl = places(k)
        p, q = swap(k, i, j)
        pick = lambda a, b: tuple(swap(k, m, n)[0] for m, n in zip(a, b))
        return p, q, pick(ar, br), pick(al, bl), pick(br, ar), pick(bl, al)

    def copy(k, n, src, dst, dev):
        return pltpu.make_async_remote_copy(
            src_ref=src,
            dst_ref=dst,
            send_sem=send_sem.at[k, SEND_SEM[n]],
            recv_sem=recv_sem.at[k, RECV_SEM[n]],
            device_id=dev,
            device_id_type=MESH,
        )

    def all_copies(k):
        i, j, ar, al, br, bl = places(k)
        i1, i2, i3 = (i + 1) % 4, (i + 2) % 4, (i + 3) % 4
        j1, j2, j3 = (j + 1) % 4, (j + 2) % 4, (j + 3) % 4
        p, q, p_right, p_left, q_right, q_left = gather_places(k)
        p1, p3, q1, q3 = (p + 1) % 4, (p + 3) % 4, (q + 1) % 4, (q + 3) % 4
        same = lambda n, ref, dev: copy(k, n, ref, ref, dev)
        near, far = pl.ds(0, 2), pl.ds(2, 2)
        return [
            lambda: copy(k, 0, terms.at[k, i2, 0], half_a.at[k, 0], ar),
            lambda: copy(k, 1, terms.at[k, i2, 1], half_a.at[k, 1], al),
            lambda: copy(k, 2, terms.at[k, i1, 1], full_a.at[k, 0, 1], ar),
            lambda: copy(k, 3, terms.at[k, i3, 0], full_a.at[k, 1, 0], al),
            lambda: copy(k, 4, terms.at[k, i1, 0], full_a.at[k, 0, 0], ar),
            lambda: copy(k, 5, terms.at[k, i3, 1], full_a.at[k, 1, 1], al),
            lambda: copy(k, 6, sums.at[k, j2, 0], half_b.at[k, 0], br),
            lambda: copy(k, 7, sums.at[k, j2, 1], half_b.at[k, 1], bl),
            lambda: copy(k, 8, sums.at[k, j1], full_b.at[k, 0], br),
            lambda: copy(k, 9, sums.at[k, j3], full_b.at[k, 1], bl),
            lambda: same(10, acts.at[k, p, q], q_right),
            lambda: same(11, acts.at[k, p, q], q_left),
            lambda: same(12, acts.at[k, p, q3, 0], q_right),
            lambda: same(13, acts.at[k, p, q1, 1], q_left),
            lambda: same(14, acts.at[k, p, near], p_right),
            lambda: same(15, acts.at[k, p, far], p_left),
            lambda: same(16, acts.at[k, p, far], p_right),
            lambda: same(17, acts.at[k, p, near], p_left),
            lambda: same(18, acts.at[k, p3, near], p_right),
            lambda: same(19, acts.at[k, p1, far], p_left),
        ]

    def arrived(k, n, ref):
        i, j, ar, al, br, bl = places(k)
        copy(k, n, ref, ref, ar).wait_recv()

    def left_here(k, n, ref):
        i, j, ar, al, br, bl = places(k)
        copy(k, n, ref, ref, ar).wait_send()

    def plus(a, b):
        return (a.astype(F32) + b.astype(F32)).astype(BF16)

    def p0(k):
        for part, (arr, weights) in enumerate(((0, w_gate), (0, w_up), (1, w_down))):
            if part < 2:
                lhs = xs[:, 0].reshape(TOKENS, WIDTH)
                val = jnp.dot(lhs, weights[k], preferred_element_type=F32)
            else:
                lhs = xs[:, 1].reshape(TOKENS, WIDTH)
                val = nt_dot(lhs, weights[k])
            val = val.astype(BF16)
            for b in range(2):
                terms[k, :, b, :, part * 16 : (part + 1) * 16, :] = val[
                    :, b * BLOCK : (b + 1) * BLOCK
                ].reshape(4, 4, 16, BLOCK)
        copies = all_copies(k)
        for n in range(4):
            copies[n]().start()

    def p1(k):
        i, j, *_ = places(k)
        i1, i3 = (i + 1) % 4, (i + 3) % 4
        copies = all_copies(k)
        arrived(k, 0, half_a.at[k])
        terms[k, i1, 0] = plus(terms[k, i1, 0], half_a[k, 0])
        copies[4]().start()
        terms[k, i3, 1] = plus(terms[k, i3, 1], half_a[k, 1])
        copies[5]().start()

    def p2(k):
        i, j, *_ = places(k)
        copies = all_copies(k)
        arrived(k, 2, full_a.at[k])
        for b in range(2):
            total = terms[k, i, b].astype(F32) + full_a[k, 0, b].astype(F32)
            sums[k, :, b] = (total + full_a[k, 1, b].astype(F32)).astype(BF16)
        copies[6]().start()
        copies[7]().start()

    def p3(k):
        i, j, *_ = places(k)
        j1, j3 = (j + 1) % 4, (j + 3) % 4
        copies = all_copies(k)
        arrived(k, 6, half_b.at[k])
        sums[k, j1, 0] = plus(sums[k, j1, 0], half_b[k, 0])
        copies[8]().start()
        sums[k, j3, 1] = plus(sums[k, j3, 1], half_b[k, 1])
        copies[9]().start()

    def p4(k):
        i, j, *_ = places(k)
        p, q, *_ = gather_places(k)
        copies = all_copies(k)
        arrived(k, 8, full_b.at[k])
        total = sums[k, j].astype(F32) + full_b[k, 0].astype(F32) + full_b[k, 1].astype(F32)
        gate, up, grad = total[:, 0:16], total[:, 16:32], total[:, 32:48]
        sigma = 1.0 / (1.0 + jnp.exp(-gate))
        acts[k, p, q, :, 0:16, :] = (gate * sigma * up).astype(BF16)
        acts[k, p, q, :, 16:32, :] = (grad * up * sigma * (1.0 + gate * (1.0 - sigma))).astype(BF16)
        acts[k, p, q, :, 32:48, :] = (grad * gate * sigma).astype(BF16)
        copies[10]().start()
        copies[11]().start()

    def p5(k):
        p, q, *_ = gather_places(k)
        copies = all_copies(k)
        arrived(k, 10, acts.at[k, p, pl.ds(0, 2)])
        copies[12]().start()
        copies[13]().start()

    def p6(k):
        p, q, *_ = gather_places(k)
        copies = all_copies(k)
        arrived(k, 12, acts.at[k, p, 0])
        for n in range(14, 18):
            copies[n]().start()

    def p7(k):
        p, q, *_ = gather_places(k)
        copies = all_copies(k)
        arrived(k, 14, acts.at[k, 0])
        copies[18]().start()
        copies[19]().start()

    def saves(at):
        return (
            pltpu.make_async_copy(hidden_t.at[at], hidden_out.at[at], save_sem.at[2]),
            pltpu.make_async_copy(pairs.at[at], pairs_out.at[at], save_sem.at[3]),
        )

    def p8(k):
        p, q, *_ = gather_places(k)
        arrived(k, 16, acts.at[k, pl.ds(0, 2)])

        groups = [swap(k, a, b) for a in range(4) for b in range(4)]

        def act(part):
            cols = [
                jnp.concatenate([acts[k, u, v, b, part * 16 : (part + 1) * 16, :] for u, v in groups])
                for b in range(2)
            ]
            return cols, jnp.concatenate(cols, axis=1)

        (_, hidden), (gate_cols, grad_gate), (up_cols, grad_up) = act(0), act(1), act(2)
        for n in range(4):
            cols = slice(n * 256, (n + 1) * 256)
            out = jnp.dot(hidden, w_down[k, :, cols], preferred_element_type=F32)
            out_acc[:, :, cols] += out.reshape(8, 32, 256)
            grad = nt_dot(grad_gate, w_gate[k, cols, :]) + nt_dot(grad_up, w_up[k, cols, :])
            gradx_acc[:, :, cols] += grad.reshape(8, 32, 256)
        hidden_t[k] = hidden.T
        for b in range(2):
            pairs[k, b, :, 0:BLOCK] = gate_cols[b]
            pairs[k, b, :, BLOCK:] = up_cols[b]
        for save in saves(k):
            save.start()
        left_here(k, 0, terms.at[k, pl.ds(0, 3)])
        left_here(k, 6, terms.at[k, pl.ds(0, 3), 0])
        left_here(k, 14, terms.at[k, pl.ds(0, 3)])

    def tick(t, carry):
        for phase, late in zip((p7, p6, p5, p4, p3, p2, p1, p0, p8), LAGS[7::-1] + LAGS[8:]):
            k = t - late

            @pl.when(jnp.logical_and(k >= 0, k < CHUNKS))
            def _():
                phase(k)

        @pl.when(t == 6)
        def _():
            lay_out_inputs()

        return carry

    lax.fori_loop(0, CHUNKS + LAGS[8], tick, 0)

    def last(n, src, dst, dev):
        return pltpu.make_async_remote_copy(
            src_ref=src,
            dst_ref=dst,
            send_sem=tail_send.at[0],
            recv_sem=tail_recv.at[n],
            device_id=dev,
            device_id_type=MESH,
        )

    x0, x1, x2, x3 = ix, (ix + 1) % 4, (ix + 2) % 4, (ix + 3) % 4
    totals = (out_acc, gradx_acc)
    cores = {}
    for n, at in ((0, x2), (1, x1), (2, x3), (3, x0)):
        for arr in range(2):
            tail_out[at, arr] = totals[arr][at * 2 + other].astype(BF16)
        cores[n] = last(n, tail_out.at[at], tail_core.at[at], sibling)
        cores[n].start()

    for n, at, ref in ((0, x2, part2_ref), (1, x1, part1_ref), (2, x3, part3_ref), (3, x0, mine_ref)):
        cores[n].wait_recv()
        for arr in range(2):
            mine = totals[arr][at * 2 + core] + tail_core[at, arr].astype(F32)
            ref[arr] = mine.astype(ref.dtype)

    last(0, tail_out, tail_core, sibling).wait_send()
    head(0, xs.at[pl.ds(0, 7)], xs.at[pl.ds(0, 7)], right).wait_send()
    save_x.wait()
    save_cots.wait()

    for save in saves(pl.ds(0, CHUNKS)):
        save.wait()


def run_layer(gate_slots, gate_count, down_slots, down_count, inputs, grad_out, gate_blocks, up_blocks, down_blocks):
    anywhere = pl.BlockSpec(memory_space=pl.ANY)
    scalars = pl.BlockSpec(memory_space=pltpu.SMEM)
    vmem = pl.BlockSpec(memory_space=pltpu.VMEM)
    raw = pltpu.VMEM((NB + 1, BLOCK, BLOCK), BF16)
    part = (48, BLOCK)
    part_of_sum = jax.ShapeDtypeStruct((2, 32, WIDTH), BF16)
    return pl.pallas_call(
        layer_kernel,
        out_shape=(
            part_of_sum,
            part_of_sum,
            part_of_sum,
            jax.ShapeDtypeStruct((2, 32, WIDTH), F32),
            jax.ShapeDtypeStruct((CHUNKS, CHUNK, TOKENS), BF16),
            jax.ShapeDtypeStruct((CHUNKS, 2, TOKENS, 2 * BLOCK), BF16),
            jax.ShapeDtypeStruct((DPB, BLOCK, TOKENS), BF16),
            jax.ShapeDtypeStruct((DPB, TOKENS, BLOCK), BF16),
        ),
        in_specs=[scalars] * 4 + [anywhere] * 5,
        out_specs=(vmem,) * 4 + (anywhere,) * 4,
        scratch_shapes=[
            pltpu.VMEM((8, 2, 32, WIDTH), BF16),
            raw,
            raw,
            raw,
            pltpu.VMEM((CHUNKS, WIDTH, CHUNK), BF16),
            pltpu.VMEM((CHUNKS, WIDTH, CHUNK), BF16),
            pltpu.VMEM((CHUNKS, CHUNK, WIDTH), BF16),
            pltpu.VMEM((CHUNKS, 4, 2, 4) + part, BF16),
            pltpu.VMEM((CHUNKS, 2, 4) + part, BF16),
            pltpu.VMEM((CHUNKS, 2, 2, 4) + part, BF16),
            pltpu.VMEM((CHUNKS, 4, 2) + part, BF16),
            pltpu.VMEM((CHUNKS, 2) + part, BF16),
            pltpu.VMEM((CHUNKS, 2, 2) + part, BF16),
            pltpu.VMEM((CHUNKS, 4, 4, 2) + part, BF16),
            pltpu.VMEM((CHUNKS, CHUNK, TOKENS), BF16),
            pltpu.VMEM((CHUNKS, 2, TOKENS, 2 * BLOCK), BF16),
            pltpu.VMEM((DPB, BLOCK, TOKENS), BF16),
            pltpu.VMEM((DPB, TOKENS, BLOCK), BF16),
            pltpu.VMEM((8, 32, WIDTH), F32),
            pltpu.VMEM((8, 32, WIDTH), F32),
            pltpu.VMEM((4, 2, 32, WIDTH), BF16),
            pltpu.VMEM((4, 2, 32, WIDTH), BF16),
            pltpu.VMEM((2, 8, 128), jnp.int32),
            pltpu.SMEM((2, 8, 128), jnp.int32),
            pltpu.SemaphoreType.DMA((6,)),
            pltpu.SemaphoreType.DMA((4,)),
            pltpu.SemaphoreType.DMA((1,)),
            pltpu.SemaphoreType.DMA((7,)),
            pltpu.SemaphoreType.DMA((CHUNKS, 3)),
            pltpu.SemaphoreType.DMA((CHUNKS, 8)),
            pltpu.SemaphoreType.DMA((1,)),
            pltpu.SemaphoreType.DMA((4,)),
        ],
        compiler_params=pltpu.CompilerParams(
            collective_id=0, has_side_effects=True, vmem_limit_bytes=60 * 2**20
        ),
        name="layer",
    )(gate_slots, gate_count, down_slots, down_count, inputs, grad_out, gate_blocks, up_blocks, down_blocks)


def grads_kernel(
    gate_slots,
    gate_count,
    down_slots,
    down_count,
    hidden_in,
    pairs_in,
    x_in,
    cots_in,
    gate_out,
    up_out,
    down_out,
    hidden_t,
    pairs,
    x_t,
    cots,
    gate_stage,
    up_stage,
    down_stage,
    load_sem,
    save_sem,
):
    loads = [
        pltpu.make_async_copy(cots_in, cots, load_sem.at[0]),
        pltpu.make_async_copy(hidden_in, hidden_t, load_sem.at[1]),
        pltpu.make_async_copy(x_in, x_t, load_sem.at[2]),
        pltpu.make_async_copy(pairs_in, pairs, load_sem.at[3]),
    ]
    for load in loads:
        load.start()
    groups = NB // GROUP

    def save(kind, stage, out, g):
        rows = pl.ds(g * GROUP, GROUP)
        return pltpu.make_async_copy(stage.at[rows], out.at[rows], save_sem.at[kind, g])

    loads[0].wait()
    loads[1].wait()

    def down_group(g, carry):
        first = g * GROUP
        live = down_count[0, 0] - first

        @pl.when(live > 0)
        def _():
            for u in range(GROUP):
                spot = down_slots[0, 0, first + u]
                val = jnp.dot(hidden_t[spot % FPB], cots[spot // FPB], preferred_element_type=F32)
                down_stage[first + u] = jnp.where(u < live, val, 0.0).astype(BF16)

        @pl.when(live <= 0)
        def _():
            down_stage[pl.ds(first, GROUP)] = jnp.zeros((GROUP, BLOCK, BLOCK), BF16)

        save(0, down_stage, down_out, g).start()
        return carry

    lax.fori_loop(0, groups, down_group, 0)
    loads[2].wait()
    loads[3].wait()

    def gate_group(g, carry):
        first = g * GROUP
        live = gate_count[0, 0] - first

        @pl.when(live > 0)
        def _():
            for u in range(GROUP):
                spot = gate_slots[0, 0, first + u]
                val = jnp.dot(x_t[spot // FPB], pairs[spot % FPB], preferred_element_type=F32)
                val = jnp.where(u < live, val, 0.0).astype(BF16)
                gate_stage[first + u] = val[:, 0:BLOCK]
                up_stage[first + u] = val[:, BLOCK:]

        @pl.when(live <= 0)
        def _():
            zero = jnp.zeros((GROUP, BLOCK, BLOCK), BF16)
            gate_stage[pl.ds(first, GROUP)] = zero
            up_stage[pl.ds(first, GROUP)] = zero

        save(1, gate_stage, gate_out, g).start()
        save(2, up_stage, up_out, g).start()
        return carry

    lax.fori_loop(0, groups, gate_group, 0)

    def finish(g, carry):
        save(0, down_stage, down_out, g).wait()
        save(1, gate_stage, gate_out, g).wait()
        save(2, up_stage, up_out, g).wait()
        return carry

    lax.fori_loop(0, groups, finish, 0)


def run_grads(gate_slots, gate_count, down_slots, down_count, hidden, pairs, x_t, cots):
    scalars = pl.BlockSpec(memory_space=pltpu.SMEM)
    anywhere = pl.BlockSpec(memory_space=pl.ANY)
    grads = jax.ShapeDtypeStruct((NB, BLOCK, BLOCK), BF16)
    return pl.pallas_call(
        grads_kernel,
        out_shape=(grads, grads, grads),
        in_specs=[scalars] * 4 + [anywhere] * 4,
        out_specs=(anywhere, anywhere, anywhere),
        scratch_shapes=[
            pltpu.VMEM((FPB, BLOCK, TOKENS), BF16),
            pltpu.VMEM((FPB, TOKENS, 2 * BLOCK), BF16),
            pltpu.VMEM((DPB, BLOCK, TOKENS), BF16),
            pltpu.VMEM((DPB, TOKENS, BLOCK), BF16),
            pltpu.VMEM((NB, BLOCK, BLOCK), BF16),
            pltpu.VMEM((NB, BLOCK, BLOCK), BF16),
            pltpu.VMEM((NB, BLOCK, BLOCK), BF16),
            pltpu.SemaphoreType.DMA((4,)),
            pltpu.SemaphoreType.DMA((3, NB // GROUP)),
        ],
        compiler_params=pltpu.CompilerParams(vmem_limit_bytes=60 * 2**20),
        cost_estimate=pl.CostEstimate(
            flops=6 * NB * BLOCK * BLOCK * TOKENS, bytes_accessed=32 * 2**20, transcendentals=0
        ),
        name="block_grads",
    )(gate_slots, gate_count, down_slots, down_count, hidden, pairs, x_t, cots)


def to_plane(value, step):
    cols = lax.axis_size("col")
    return lax.ppermute(value, "col", [(c, (c + 2 * step) % cols) for c in range(cols)])


def local(
    inputs,
    grad_out,
    gate_blocks,
    up_blocks,
    down_blocks,
    gate_slots,
    gate_count,
    down_slots,
    down_count,
):
    part1, part2, part3, mine, hidden, pairs, x_t, cots = run_layer(
        gate_slots,
        gate_count,
        down_slots,
        down_count,
        inputs,
        grad_out,
        gate_blocks[0, 0],
        up_blocks[0, 0],
        down_blocks[0, 0],
    )
    arrived = [to_plane(part2, 2), to_plane(part1, 1), to_plane(part3, 3)]
    hidden = hidden.reshape(FPB, BLOCK, TOKENS)
    pairs = pairs.reshape(FPB, TOKENS, 2 * BLOCK)
    grads = run_grads(gate_slots, gate_count, down_slots, down_count, hidden, pairs, x_t, cots)
    total = mine + sum(part.astype(F32) for part in arrived)
    layer_out, grad_x = total[0].astype(BF16), total[1].astype(BF16)
    return (layer_out, grad_x) + tuple(grad[None, None] for grad in grads)


def solution(mesh):
    tokens = P("col", "row")
    blocks = P("row", "col", None, None, None)
    slots = P("row", "col", None)
    count = P("row", "col")
    return jax.shard_map(
        local,
        mesh=mesh,
        in_specs=(tokens, tokens, blocks, blocks, blocks, slots, count, slots, count),
        out_specs=(tokens, tokens, blocks, blocks, blocks),
        check_vma=False,
    )
```

time: 103 us -> 97 us (0.942)
  Pallas kernels: 98.1 us -> 90 us
  starting transfers between devices: 0 us -> 4.11 us
  other arithmetic: 1.97 us -> 0.06 us
    pallas_call x2, Pallas kernels: 98.1 us -> 90 us  [the longest x1 81.7 us: run_layer(): pl.pallas_call(layer_kernel, out_shape=(part_of_sum, part_of_sum, part_of...]
    ppermute x0 -> x3, starting transfers between devices: none -> 4.11 us  [to_plane(): lax.ppermute(value, 'col', [(c, (c + 2 * step) % cols) for c in range(col...]
    reduce_min x1 -> x0, other arithmetic: 1.37 us -> none  [slot_of(): return jnp.min(jnp.where(hit, ids[None, :], NB), axis=1)]
  transfers between devices with their start and end apart: 0 -> 3, of which waited for: 0 -> 0; matrix products, arithmetic and copies ran while one was open for 0% -> 0% of each run, Pallas kernels for 0% -> 9%
where the time goes in v2:
time: 97 us; the launch traced here: 96.9 us
  Pallas kernels  90 us (93%)
  starting transfers between devices  4.11 us (4%)
  between operations  1.98 us (2%)
    pallas_call x1, Pallas kernels, run_layer(): pl.pallas_call(layer_kernel, out_shape=(part_of_sum, part_of_sum, part_of...  81.7 us
    pallas_call x1, Pallas kernels, run_grads(): pl.pallas_call(grads_kernel, out_shape=(grads, grads, grads), in_specs=[s...  8.36 us
    ppermute x3, starting transfers between devices, to_plane(): lax.ppermute(value, 'col', [(c, (c + 2 * step) % cols) for c in range(col...  4.11 us
  transfers between devices with their start and end apart: 3, of which 0 were waited for; matrix products, arithmetic and copies ran while one was open for 0% of the time, Pallas kernels for 9%

profile of v2, /device:TPU:1, one launch (start us, length us, event | category | flops | bytes accessed | tf_op | source)
XLA Modules:
  0.0 96.9 jit_solution(17644857065923607106)
XLA Ops:
  1.9 81.7 %layer.1 = (bf16[2,32,1024]{2,1,0:T(8,128)(2,1)}, bf16[2,32,1024]{2,1,0:T(8,128)(2,1)}, bf16[2,32,1024]{2,1,0:T(8,128)(2,1)}, f32[2,32,1024]{2,1,0:T(8,128)}, bf...) custom-call(s32[1,1,96]{2,1,0:T(1,128)} %gate_slots.3, ...), custom_call_target="tpu_custom_call" | custom-call | tf_op jit(solution)/shard_map/layer/pallas_call | solution.py:482
  83.6 1.4 %collective-permute-start = (bf16[2,32,1024]{2,1,0:T(8,128)(2,1)}, bf16[2,32,1024]{2,1,0:T(8,128)(2,1)S(1)}, u32[]{:S(2)}, u32[]{:S(2)}) collective-permute-start(bf16[2,32,1024]{2,1,0:T(8,128)(2,1)} %get-tuple-element.17), channel_id=1, source_target_pairs={{0,4},{1,5},{2,6},{3,7},{4,0},{5,1},{6,2},{7,3},{8,12},{9,13},{10,... | collective-permute-start | bytes 393224 | tf_op jit(solution)/shard_map/ppermute | solution.py:662
  85.0 0.6 collective-permute-start.1
  85.7 2.0 %collective-permute-start.2 = (bf16[2,32,1024]{2,1,0:T(8,128)(2,1)}, bf16[2,32,1024]{2,1,0:T(8,128)(2,1)S(1)}, u32[]{:S(2)}, u32[]{:S(2)}) collective-permute-start(bf16[2,32,1024]{2,1,0:T(8,128)(2,1)} %get-tuple-element.19), channel_id=1, source_target_pairs={{0,6},{1,7},{2,0},{3,1},{4,2},{5,3},{6,4},{7,5},{8,14},{9,15},{10,... | collective-permute-start | bytes 393224 | tf_op jit(solution)/shard_map/ppermute | solution.py:662
  87.7 0.0 copy-start
  87.7 8.4 %block_grads.1 = (bf16[96,128,128]{2,1,0:T(8,128)(2,1)}, bf16[96,128,128]{2,1,0:T(8,128)(2,1)}, bf16[96,128,128]{2,1,0:T(8,128)(2,1)}) custom-call(s32[1,1,96]{2,1,0:T(1,128)} %gate_slots.3, s32[1,1]{1,0:T(1,128)S(6)} %copy.14.gate_count, s32[1,1,96]{2,1,0:T(1,128)} %down_slots.3, s32[1,1]{1,0:T(1,128)S(6)} %copy.15.down_count, ...), custom_call_target="tpu_custom_call" | custom-call | flops 2415919104 | bytes 33554432 | tf_op jit(solution)/shard_map/block_grads/pallas_call | solution.py:636
  96.1 0.0 collective-permute-done
  96.1 0.0 collective-permute-done.1
  96.1 0.0 collective-permute-done.2
  96.1 0.0 copy-done
  96.1 0.1 add_convert_fusion
  96.2 0.7 slice_bitcast_fusion
Async XLA Ops:
  83.6 12.5 %collective-permute-start = (bf16[2,32,1024]{2,1,0:T(8,128)(2,1)}, bf16[2,32,1024]{2,1,0:T(8,128)(2,1)S(1)}, u32[]{:S(2)}, u32[]{:S(2)}) collective-permute-start(bf16[2,32,1024]{2,1,0:T(8,128)(2,1)} %get-tuple-element.17), channel_id=1, source_target_pairs={{0,4},{1,5},{2,6},{3,7},{4,0},{5,1},{6,2},{7,3},{8,12},{9,13},{10,... | collective-permute-start | bytes 393224 | tf_op jit(solution)/shard_map/ppermute | solution.py:662
  85.0 11.1 %collective-permute-start.1 = (bf16[2,32,1024]{2,1,0:T(8,128)(2,1)}, bf16[2,32,1024]{2,1,0:T(8,128)(2,1)S(1)}, u32[]{:S(2)}, u32[]{:S(2)}) collective-permute-start(bf16[2,32,1024]{2,1,0:T(8,128)(2,1)} %get-tuple-element.18), channel_id=1, source_target_pairs={{0,2},{1,3},{2,4},{3,5},{4,6},{5,7},{6,0},{7,1},{8,10},{9,11},{10,... | collective-permute-start | bytes 393224 | tf_op jit(solution)/shard_map/ppermute | solution.py:662
  85.7 10.4 %collective-permute-start.2 = (bf16[2,32,1024]{2,1,0:T(8,128)(2,1)}, bf16[2,32,1024]{2,1,0:T(8,128)(2,1)S(1)}, u32[]{:S(2)}, u32[]{:S(2)}) collective-permute-start(bf16[2,32,1024]{2,1,0:T(8,128)(2,1)} %get-tuple-element.19), channel_id=1, source_target_pairs={{0,6},{1,7},{2,0},{3,1},{4,2},{5,3},{6,4},{7,5},{8,14},{9,15},{10,... | collective-permute-start | bytes 393224 | tf_op jit(solution)/shard_map/ppermute | solution.py:662
  87.7 8.4 %copy-start = (f32[2,32,1024]{2,1,0:T(8,128)S(1)}, f32[2,32,1024]{2,1,0:T(8,128)}, u32[]{:S(2)}) copy-start(f32[2,32,1024]{2,1,0:T(8,128)} %get-tuple-element.16) | copy-start | bytes 786436

commit v3 on v2

--- a/solution.py
+++ b/solution.py
@@ -16,6 +16,8 @@
 GROUP = 16
 LAGS = (0, 4, 8, 12, 16, 20, 24, 28, 32)
 MESH = pl.DeviceIdType.MESH
+TAIL_SEND = (0,) * 4 + (1,) * 6
+TAIL_RECV = (0, 1, 2, 3, 4, 5) + (6,) * 4
 HEAD_SEM = (0, 1, 2, 3, 6, 6, 4, 6, 5, 6, 6, 6, 6, 6)
 SEND_SEM = (0,) * 6 + (1,) * 8 + (2,) * 6
 RECV_SEM = (0, 0, 1, 1, 1, 1, 2, 2, 3, 3, 4, 4, 5, 5, 6, 6, 7, 7, 7, 7)
@@ -37,18 +39,11 @@
     gate_in,
     up_in,
     down_in,
-    part1_ref,
-    part2_ref,
-    part3_ref,
-    mine_ref,
-    hidden_out,
-    pairs_out,
-    x_out,
-    cots_out,
-    xs,
+    layer_ref,
     raw_gate,
     raw_up,
     raw_down,
+    xs,
     w_gate,
     w_up,
     w_down,
@@ -66,11 +61,13 @@
     out_acc,
     gradx_acc,
     tail_out,
+    tail,
     tail_core,
+    tail_h,
+    tail_f,
     tables,
     slot_at,
     load_sem,
-    save_sem,
     head_send,
     head_recv,
     send_sem,
@@ -219,16 +216,11 @@
     loads[0].wait()
     loads[1].wait()
 
-    save_x = pltpu.make_async_copy(x_t, x_out, save_sem.at[0])
-    save_cots = pltpu.make_async_copy(cots, cots_out, save_sem.at[1])
-
     def lay_out_inputs():
         for r in range(DPB):
             cols = slice(r * BLOCK, (r + 1) * BLOCK)
             x_t[r] = xs[:, 0, :, cols].reshape(TOKENS, BLOCK).T
             cots[r] = xs[:, 1, :, cols].reshape(TOKENS, BLOCK)
-        save_x.start()
-        save_cots.start()
 
     def places(k):
         odd = k % 2
@@ -386,12 +378,6 @@
         copies[18]().start()
         copies[19]().start()
 
-    def saves(at):
-        return (
-            pltpu.make_async_copy(hidden_t.at[at], hidden_out.at[at], save_sem.at[2]),
-            pltpu.make_async_copy(pairs.at[at], pairs_out.at[at], save_sem.at[3]),
-        )
-
     def p8(k):
         p, q, *_ = gather_places(k)
         arrived(k, 16, acts.at[k, pl.ds(0, 2)])
@@ -412,12 +398,10 @@
             out_acc[:, :, cols] += out.reshape(8, 32, 256)
             grad = nt_dot(grad_gate, w_gate[k, cols, :]) + nt_dot(grad_up, w_up[k, cols, :])
             gradx_acc[:, :, cols] += grad.reshape(8, 32, 256)
-        hidden_t[k] = hidden.T
+        hidden_t[pl.ds(2 * k, 2)] = hidden.T.reshape(2, BLOCK, TOKENS)
         for b in range(2):
-            pairs[k, b, :, 0:BLOCK] = gate_cols[b]
-            pairs[k, b, :, BLOCK:] = up_cols[b]
-        for save in saves(k):
-            save.start()
+            pairs[2 * k + b, :, 0:BLOCK] = gate_cols[b]
+            pairs[2 * k + b, :, BLOCK:] = up_cols[b]
         left_here(k, 0, terms.at[k, pl.ds(0, 3)])
         left_here(k, 6, terms.at[k, pl.ds(0, 3), 0])
         left_here(k, 14, terms.at[k, pl.ds(0, 3)])
@@ -437,13 +421,31 @@
         return carry
 
     lax.fori_loop(0, CHUNKS + LAGS[8], tick, 0)
+
+    def down_group(g, carry):
+        for u in range(GROUP):
+            n = g * GROUP + u
+            spot = down_slots[0, 0, n]
+            val = jnp.dot(hidden_t[spot % FPB], cots[spot // FPB], preferred_element_type=F32)
+            raw_down[n] = jnp.where(n < down_count[0, 0], val, 0.0).astype(BF16)
+        return carry
+
+    def gate_group(g, carry):
+        for u in range(GROUP):
+            n = g * GROUP + u
+            spot = gate_slots[0, 0, n]
+            val = jnp.dot(x_t[spot // FPB], pairs[spot % FPB], preferred_element_type=F32)
+            val = jnp.where(n < gate_count[0, 0], val, 0.0).astype(BF16)
+            raw_gate[n] = val[:, 0:BLOCK]
+            raw_up[n] = val[:, BLOCK:]
+        return carry
 
     def last(n, src, dst, dev):
         return pltpu.make_async_remote_copy(
             src_ref=src,
             dst_ref=dst,
-            send_sem=tail_send.at[0],
-            recv_sem=tail_recv.at[n],
+            send_sem=tail_send.at[TAIL_SEND[n]],
+            recv_sem=tail_recv.at[TAIL_RECV[n]],
             device_id=dev,
             device_id_type=MESH,
         )
@@ -457,19 +459,47 @@
         cores[n] = last(n, tail_out.at[at], tail_core.at[at], sibling)
         cores[n].start()
 
-    for n, at, ref in ((0, x2, part2_ref), (1, x1, part1_ref), (2, x3, part3_ref), (3, x0, mine_ref)):
+    def both(n, at):
         cores[n].wait_recv()
         for arr in range(2):
             mine = totals[arr][at * 2 + core] + tail_core[at, arr].astype(F32)
-            ref[arr] = mine.astype(ref.dtype)
+            tail[at, arr] = mine.astype(BF16)
+
+    steps = [
+        last(4, tail.at[x2, 0], tail_h.at[0], right),
+        last(5, tail.at[x2, 1], tail_h.at[1], left),
+        last(6, tail.at[x1, 1], tail_f.at[0, 1], right),
+        last(7, tail.at[x3, 0], tail_f.at[1, 0], left),
+        last(8, tail.at[x1, 0], tail_f.at[0, 0], right),
+        last(9, tail.at[x3, 1], tail_f.at[1, 1], left),
+    ]
+    lax.fori_loop(0, 2, down_group, 0)
+    both(0, x2)
+    steps[0].start()
+    steps[1].start()
+    both(1, x1)
+    steps[2].start()
+    both(2, x3)
+    steps[3].start()
+    lax.fori_loop(2, 6, down_group, 0)
+    lax.fori_loop(0, 3, gate_group, 0)
+    steps[0].wait_recv()
+    tail[x1, 0] = plus(tail[x1, 0], tail_h[0])
+    steps[4].start()
+    steps[1].wait_recv()
+    tail[x3, 1] = plus(tail[x3, 1], tail_h[1])
+    steps[5].start()
+    lax.fori_loop(3, 6, gate_group, 0)
+    cores[3].wait_recv()
+    last(6, tail_f, tail_f, right).wait_recv()
+    for arr in range(2):
+        total = totals[arr][x0 * 2 + core] + tail_core[x0, arr].astype(F32)
+        total = total + tail_f[0, arr].astype(F32) + tail_f[1, arr].astype(F32)
+        layer_ref[arr] = total.astype(BF16)
 
     last(0, tail_out, tail_core, sibling).wait_send()
+    last(4, tail.at[pl.ds(0, 3)], tail.at[pl.ds(0, 3)], right).wait_send()
     head(0, xs.at[pl.ds(0, 7)], xs.at[pl.ds(0, 7)], right).wait_send()
-    save_x.wait()
-    save_cots.wait()
-
-    for save in saves(pl.ds(0, CHUNKS)):
-        save.wait()
 
 
 def run_layer(gate_slots, gate_count, down_slots, down_count, inputs, grad_out, gate_blocks, up_blocks, down_blocks):
@@ -478,26 +508,18 @@
     vmem = pl.BlockSpec(memory_space=pltpu.VMEM)
     raw = pltpu.VMEM((NB + 1, BLOCK, BLOCK), BF16)
     part = (48, BLOCK)
-    part_of_sum = jax.ShapeDtypeStruct((2, 32, WIDTH), BF16)
     return pl.pallas_call(
         layer_kernel,
         out_shape=(
-            part_of_sum,
-            part_of_sum,
-            part_of_sum,
-            jax.ShapeDtypeStruct((2, 32, WIDTH), F32),
-            jax.ShapeDtypeStruct((CHUNKS, CHUNK, TOKENS), BF16),
-            jax.ShapeDtypeStruct((CHUNKS, 2, TOKENS, 2 * BLOCK), BF16),
-            jax.ShapeDtypeStruct((DPB, BLOCK, TOKENS), BF16),
-            jax.ShapeDtypeStruct((DPB, TOKENS, BLOCK), BF16),
-        ),
-        in_specs=[scalars] * 4 + [anywhere] * 5,
-        out_specs=(vmem,) * 4 + (anywhere,) * 4,
-        scratch_shapes=[
-            pltpu.VMEM((8, 2, 32, WIDTH), BF16),
+            pltpu.VMEM((2, 32, WIDTH), BF16),
             raw,
             raw,
             raw,
+        ),
+        in_specs=[scalars] * 4 + [anywhere] * 5,
+        out_specs=(vmem,) * 4,
+        scratch_shapes=[
+            pltpu.VMEM((8, 2, 32, WIDTH), BF16),
             pltpu.VMEM((CHUNKS, WIDTH, CHUNK), BF16),
             pltpu.VMEM((CHUNKS, WIDTH, CHUNK), BF16),
             pltpu.VMEM((CHUNKS, CHUNK, WIDTH), BF16),
@@ -508,158 +530,64 @@
             pltpu.VMEM((CHUNKS, 2) + part, BF16),
             pltpu.VMEM((CHUNKS, 2, 2) + part, BF16),
             pltpu.VMEM((CHUNKS, 4, 4, 2) + part, BF16),
-            pltpu.VMEM((CHUNKS, CHUNK, TOKENS), BF16),
-            pltpu.VMEM((CHUNKS, 2, TOKENS, 2 * BLOCK), BF16),
+            pltpu.VMEM((FPB, BLOCK, TOKENS), BF16),
+            pltpu.VMEM((FPB, TOKENS, 2 * BLOCK), BF16),
             pltpu.VMEM((DPB, BLOCK, TOKENS), BF16),
             pltpu.VMEM((DPB, TOKENS, BLOCK), BF16),
             pltpu.VMEM((8, 32, WIDTH), F32),
             pltpu.VMEM((8, 32, WIDTH), F32),
             pltpu.VMEM((4, 2, 32, WIDTH), BF16),
             pltpu.VMEM((4, 2, 32, WIDTH), BF16),
+            pltpu.VMEM((4, 2, 32, WIDTH), BF16),
+            pltpu.VMEM((2, 32, WIDTH), BF16),
+            pltpu.VMEM((2, 2, 32, WIDTH), BF16),
             pltpu.VMEM((2, 8, 128), jnp.int32),
             pltpu.SMEM((2, 8, 128), jnp.int32),
             pltpu.SemaphoreType.DMA((6,)),
-            pltpu.SemaphoreType.DMA((4,)),
             pltpu.SemaphoreType.DMA((1,)),
             pltpu.SemaphoreType.DMA((7,)),
             pltpu.SemaphoreType.DMA((CHUNKS, 3)),
             pltpu.SemaphoreType.DMA((CHUNKS, 8)),
-            pltpu.SemaphoreType.DMA((1,)),
-            pltpu.SemaphoreType.DMA((4,)),
+            pltpu.SemaphoreType.DMA((2,)),
+            pltpu.SemaphoreType.DMA((7,)),
         ],
         compiler_params=pltpu.CompilerParams(
-            collective_id=0, has_side_effects=True, vmem_limit_bytes=60 * 2**20
+            collective_id=0, has_side_effects=True, vmem_limit_bytes=51 * 2**20
         ),
         name="layer",
     )(gate_slots, gate_count, down_slots, down_count, inputs, grad_out, gate_blocks, up_blocks, down_blocks)
 
 
-def grads_kernel(
-    gate_slots,
-    gate_count,
-    down_slots,
-    down_count,
-    hidden_in,
-    pairs_in,
-    x_in,
-    cots_in,
-    gate_out,
-    up_out,
-    down_out,
-    hidden_t,
-    pairs,
-    x_t,
-    cots,
-    gate_stage,
-    up_stage,
-    down_stage,
-    load_sem,
-    save_sem,
+def save_kernel(
+    layer, gate, up, down, out_ref, gradx_ref, gate_out, up_out, down_out, sem
 ):
-    loads = [
-        pltpu.make_async_copy(cots_in, cots, load_sem.at[0]),
-        pltpu.make_async_copy(hidden_in, hidden_t, load_sem.at[1]),
-        pltpu.make_async_copy(x_in, x_t, load_sem.at[2]),
-        pltpu.make_async_copy(pairs_in, pairs, load_sem.at[3]),
+    pairs = ((gate, gate_out), (up, up_out), (down, down_out))
+    saves = [
+        pltpu.make_async_copy(here.at[pl.ds(0, NB)], out, sem.at[n])
+        for n, (here, out) in enumerate(pairs)
     ]
-    for load in loads:
-        load.start()
-    groups = NB // GROUP
-
-    def save(kind, stage, out, g):
-        rows = pl.ds(g * GROUP, GROUP)
-        return pltpu.make_async_copy(stage.at[rows], out.at[rows], save_sem.at[kind, g])
-
-    loads[0].wait()
-    loads[1].wait()
-
-    def down_group(g, carry):
-        first = g * GROUP
-        live = down_count[0, 0] - first
-
-        @pl.when(live > 0)
-        def _():
-            for u in range(GROUP):
-                spot = down_slots[0, 0, first + u]
-                val = jnp.dot(hidden_t[spot % FPB], cots[spot // FPB], preferred_element_type=F32)
-                down_stage[first + u] = jnp.where(u < live, val, 0.0).astype(BF16)
-
-        @pl.when(live <= 0)
-        def _():
-            down_stage[pl.ds(first, GROUP)] = jnp.zeros((GROUP, BLOCK, BLOCK), BF16)
-
-        save(0, down_stage, down_out, g).start()
-        return carry
-
-    lax.fori_loop(0, groups, down_group, 0)
-    loads[2].wait()
-    loads[3].wait()
-
-    def gate_group(g, carry):
-        first = g * GROUP
-        live = gate_count[0, 0] - first
-
-        @pl.when(live > 0)
-        def _():
-            for u in range(GROUP):
-                spot = gate_slots[0, 0, first + u]
-                val = jnp.dot(x_t[spot // FPB], pairs[spot % FPB], preferred_element_type=F32)
-                val = jnp.where(u < live, val, 0.0).astype(BF16)
-                gate_stage[first + u] = val[:, 0:BLOCK]
-                up_stage[first + u] = val[:, BLOCK:]
-
-        @pl.when(live <= 0)
-        def _():
-            zero = jnp.zeros((GROUP, BLOCK, BLOCK), BF16)
-            gate_stage[pl.ds(first, GROUP)] = zero
-            up_stage[pl.ds(first, GROUP)] = zero
-
-        save(1, gate_stage, gate_out, g).start()
-        save(2, up_stage, up_out, g).start()
-        return carry
-
-    lax.fori_loop(0, groups, gate_group, 0)
-
-    def finish(g, carry):
-        save(0, down_stage, down_out, g).wait()
-        save(1, gate_stage, gate_out, g).wait()
-        save(2, up_stage, up_out, g).wait()
-        return carry
-
-    lax.fori_loop(0, groups, finish, 0)
-
-
-def run_grads(gate_slots, gate_count, down_slots, down_count, hidden, pairs, x_t, cots):
-    scalars = pl.BlockSpec(memory_space=pltpu.SMEM)
+    for save in saves:
+        save.start()
+    out_ref[...] = layer[0]
+    gradx_ref[...] = layer[1]
+    for save in saves:
+        save.wait()
+
+
+def run_save(layer, *grads):
+    vmem = pl.BlockSpec(memory_space=pltpu.VMEM)
     anywhere = pl.BlockSpec(memory_space=pl.ANY)
-    grads = jax.ShapeDtypeStruct((NB, BLOCK, BLOCK), BF16)
+    tokens = jax.ShapeDtypeStruct((32, WIDTH), BF16)
+    blocks = jax.ShapeDtypeStruct((NB, BLOCK, BLOCK), BF16)
     return pl.pallas_call(
-        grads_kernel,
-        out_shape=(grads, grads, grads),
-        in_specs=[scalars] * 4 + [anywhere] * 4,
-        out_specs=(anywhere, anywhere, anywhere),
-        scratch_shapes=[
-            pltpu.VMEM((FPB, BLOCK, TOKENS), BF16),
-            pltpu.VMEM((FPB, TOKENS, 2 * BLOCK), BF16),
-            pltpu.VMEM((DPB, BLOCK, TOKENS), BF16),
-            pltpu.VMEM((DPB, TOKENS, BLOCK), BF16),
-            pltpu.VMEM((NB, BLOCK, BLOCK), BF16),
-            pltpu.VMEM((NB, BLOCK, BLOCK), BF16),
-            pltpu.VMEM((NB, BLOCK, BLOCK), BF16),
-            pltpu.SemaphoreType.DMA((4,)),
-            pltpu.SemaphoreType.DMA((3, NB // GROUP)),
-        ],
-        compiler_params=pltpu.CompilerParams(vmem_limit_bytes=60 * 2**20),
-        cost_estimate=pl.CostEstimate(
-            flops=6 * NB * BLOCK * BLOCK * TOKENS, bytes_accessed=32 * 2**20, transcendentals=0
-        ),
-        name="block_grads",
-    )(gate_slots, gate_count, down_slots, down_count, hidden, pairs, x_t, cots)
-
-
-def to_plane(value, step):
-    cols = lax.axis_size("col")
-    return lax.ppermute(value, "col", [(c, (c + 2 * step) % cols) for c in range(cols)])
+        save_kernel,
+        out_shape=(tokens, tokens, blocks, blocks, blocks),
+        in_specs=[vmem] + [anywhere] * 3,
+        out_specs=(vmem, vmem, anywhere, anywhere, anywhere),
+        scratch_shapes=[pltpu.SemaphoreType.DMA((3,))],
+        compiler_params=pltpu.CompilerParams(vmem_limit_bytes=16 * 2**20),
+        name="save",
+    )(layer, *grads)
 
 
 def local(
@@ -673,7 +601,7 @@
     down_slots,
     down_count,
 ):
-    part1, part2, part3, mine, hidden, pairs, x_t, cots = run_layer(
+    layer, *grads = run_layer(
         gate_slots,
         gate_count,
         down_slots,
@@ -684,12 +612,7 @@
         up_blocks[0, 0],
         down_blocks[0, 0],
     )
-    arrived = [to_plane(part2, 2), to_plane(part1, 1), to_plane(part3, 3)]
-    hidden = hidden.reshape(FPB, BLOCK, TOKENS)
-    pairs = pairs.reshape(FPB, TOKENS, 2 * BLOCK)
-    grads = run_grads(gate_slots, gate_count, down_slots, down_count, hidden, pairs, x_t, cots)
-    total = mine + sum(part.astype(F32) for part in arrived)
-    layer_out, grad_x = total[0].astype(BF16), total[1].astype(BF16)
+    layer_out, grad_x, *grads = run_save(layer, *grads)
     return (layer_out, grad_x) + tuple(grad[None, None] for grad in grads)
 
 

time: 97 us -> 94.1 us (0.970)
  starting transfers between devices: 4.11 us -> 0 us
  Pallas kernels: 90 us -> 92 us
    ppermute x3 -> x0, starting transfers between devices: 4.11 us -> none  [to_plane(): lax.ppermute(value, 'col', [(c, (c + 2 * step) % cols) for c in range(col...]
    pallas_call x2, Pallas kernels: 90 us -> 92 us  [the longest x1 87.6 us: run_layer(): pl.pallas_call(layer_kernel, out_shape=(pltpu.VMEM((2, 32, WIDTH), BF16),...]
  transfers between devices with their start and end apart: 3 -> 0, of which waited for: 0 -> 0; matrix products, arithmetic and copies ran while one was open for 0% -> 0% of each run, Pallas kernels for 9% -> 0%
where the time goes in v3:
time: 94.1 us; the launch traced here: 94 us
  Pallas kernels  92 us (98%)
  between operations  1.93 us (2%)
    pallas_call x1, Pallas kernels, run_layer(): pl.pallas_call(layer_kernel, out_shape=(pltpu.VMEM((2, 32, WIDTH), BF16),...  87.6 us
    pallas_call x1, Pallas kernels, run_save(): pl.pallas_call(save_kernel, out_shape=(tokens, tokens, blocks, blocks, bl...  4.41 us

profile of v3, /device:TPU:1, one launch (start us, length us, event | category | flops | bytes accessed | tf_op | source)
XLA Modules:
  0.0 94.0 jit_solution(7823015910399327791)
XLA Ops:
  1.9 87.6 %layer.1 = (bf16[2,32,1024]{2,1,0:T(8,128)(2,1)S(1)}, bf16[97,128,128]{2,1,0:T(8,128)(2,1)S(1)}, bf16[97,128,128]{2,1,0:T(8,128)(2,1)S(1)}, bf16[97,128,128]{2,1,0:T(8,128)(2,1)S(1)}) custom-call(s32[1,1,96]{2,1,0:T(1,128)} %gate_slots.1, s32[1,1]{1,0:T(1,128)S(6)} %copy.14.gate_count, s32[1,1,96]{2,1,0:T(1,128)} %down_slots.1, s32[1,1]{1,0:T(1,128)S(6)} %copy.15.down_count, ...), custom_call_target="tpu_custom_call" | custom-call | tf_op jit(solution)/shard_map/layer/pallas_call | solution.py:511
  89.6 4.4 %save.1 = (bf16[32,1024]{1,0:T(8,128)(2,1)}, bf16[32,1024]{1,0:T(8,128)(2,1)}, bf16[96,128,128]{2,1,0:T(8,128)(2,1)}, bf16[96,128,128]{2,1,0:T(8,128)(2,1)}, bf16[96,128,128]{2,1,0:T(8,128)(2,1)}) custom-call(bf16[2,32,1024]{2,1,0:T(8,128)(2,1)S(1)} %get-tuple-element.14.layer, bf16[97,128,128]{2,1,0:T(8,128)(2,1)S(1)} %get-tuple-element.15.gate, ...), custom_call_target="tpu_custom_call" | custom-call | tf_op jit(solution)/shard_map/save/pallas_call | solution.py:582

commit v4 on v3

--- a/solution.py
+++ b/solution.py
@@ -14,11 +14,12 @@
 CHUNK = 2 * BLOCK
 CHUNKS = FPB // 2
 GROUP = 16
+FAR_BIG, FAR_SMALL = 13, 13
 LAGS = (0, 4, 8, 12, 16, 20, 24, 28, 32)
 MESH = pl.DeviceIdType.MESH
-TAIL_SEND = (0,) * 4 + (1,) * 6
-TAIL_RECV = (0, 1, 2, 3, 4, 5) + (6,) * 4
-HEAD_SEM = (0, 1, 2, 3, 6, 6, 4, 6, 5, 6, 6, 6, 6, 6)
+TAIL_SEND = (0,) * 4 + (1,) * 8
+TAIL_RECV = tuple(range(8)) + (8,) * 4
+HEAD_SEM = (0, 1, 2, 3, 4, 5, 8, 8, 6, 7, 6, 7) + (8,) * 6
 SEND_SEM = (0,) * 6 + (1,) * 8 + (2,) * 6
 RECV_SEM = (0, 0, 1, 1, 1, 1, 2, 2, 3, 3, 4, 4, 5, 5, 6, 6, 7, 7, 7, 7)
 F32 = jnp.float32
@@ -126,8 +127,8 @@
     other = 1 - core
     right, left = x_dev(1), x_dev(3)
 
-    def at_x(step, side, arr):
-        return xs.at[((ix + step) % 4) * 2 + side, arr]
+    def at_x(step, side, arr, rows=pl.ds(0, 32)):
+        return xs.at[((ix + step) % 4) * 2 + side, arr, rows]
 
     def head_start(n, src, dst, dev):
         head(n, src, dst, dev).start()
@@ -138,12 +139,15 @@
     def head_wait(n, ref):
         head(n, ref, ref, right).wait_recv()
 
-    head_start(0, x_in, xs.at[col, 0], right)
-    head_start(1, cot_in, xs.at[col, 1], left)
-    head_start(2, cot_in, xs.at[col, 1], right)
-    head_start(3, x_in, xs.at[col, 0], left)
-    head_start(4, x_in, xs.at[col, 0], sibling)
-    head_start(5, cot_in, xs.at[col, 1], sibling)
+    first, second = pl.ds(0, 16), pl.ds(16, 16)
+    head_start(0, x_in.at[first], xs.at[col, 0, first], right)
+    head_start(1, cot_in.at[first], xs.at[col, 1, first], left)
+    head_start(2, x_in.at[second], xs.at[col, 0, second], right)
+    head_start(3, cot_in.at[second], xs.at[col, 1, second], left)
+    head_start(4, cot_in, xs.at[col, 1], right)
+    head_start(5, x_in, xs.at[col, 0], left)
+    head_start(6, x_in, xs.at[col, 0], sibling)
+    head_start(7, cot_in, xs.at[col, 1], sibling)
     for load in loads[2:]:
         load.start()
 
@@ -187,32 +191,36 @@
     loads[3].wait()
     lax.fori_loop(0, 4, place_gate, 0)
 
-    head_wait(0, at_x(3, core, 0))
-    forward(6, at_x(3, core, 0), right)
-    forward(7, at_x(3, core, 0), sibling)
-    head_wait(1, at_x(1, core, 1))
-    forward(8, at_x(1, core, 1), left)
-    forward(9, at_x(1, core, 1), sibling)
+    head_wait(0, at_x(3, core, 0, first))
+    forward(8, at_x(3, core, 0, first), right)
+    head_wait(1, at_x(1, core, 1, first))
+    forward(9, at_x(1, core, 1, first), left)
+    head_wait(2, at_x(3, core, 0, second))
+    forward(10, at_x(3, core, 0, second), right)
+    forward(12, at_x(3, core, 0), sibling)
+    head_wait(3, at_x(1, core, 1, second))
+    forward(11, at_x(1, core, 1, second), left)
+    forward(13, at_x(1, core, 1), sibling)
 
     lax.fori_loop(4, 8, place_gate, 0)
 
-    head_wait(2, at_x(3, core, 1))
-    forward(10, at_x(3, core, 1), sibling)
-    head_wait(3, at_x(1, core, 0))
-    forward(11, at_x(1, core, 0), sibling)
+    head_wait(4, at_x(3, core, 1))
+    forward(14, at_x(3, core, 1), sibling)
+    head_wait(5, at_x(1, core, 0))
+    forward(15, at_x(1, core, 0), sibling)
 
     lax.fori_loop(8, CHUNKS, place_gate, 0)
     loads[4].wait()
     lax.fori_loop(0, 4, place_down, 0)
 
-    head_wait(6, at_x(2, core, 0))
-    forward(12, at_x(2, core, 0), sibling)
-    head_wait(8, at_x(2, core, 1))
-    forward(13, at_x(2, core, 1), sibling)
+    head_wait(8, at_x(2, core, 0))
+    forward(16, at_x(2, core, 0), sibling)
+    head_wait(9, at_x(2, core, 1))
+    forward(17, at_x(2, core, 1), sibling)
 
     lax.fori_loop(4, CHUNKS, place_down, 0)
 
-    head_wait(4, xs.at[pl.ds(0, 4)])
+    head_wait(6, xs.at[pl.ds(0, 4)])
     loads[0].wait()
     loads[1].wait()
 
@@ -234,6 +242,10 @@
 
         return i, j, dev(1, odd), dev(3, odd), dev(1, 1 - odd), dev(3, 1 - odd)
 
+    def far(k, along_a):
+        along_z = swap(k, k % 2, 1 - k % 2)[1 - along_a]
+        return ((z + 2 * along_z) % 4 * 4 + (y + 2 * (1 - along_z)) % 4, col)
+
     def swap(k, a, b):
         turned = k // (CHUNKS - 1)
         return (1 - turned) * a + turned * b, (1 - turned) * b + turned * a
@@ -244,11 +256,16 @@
         pick = lambda a, b: tuple(swap(k, m, n)[0] for m, n in zip(a, b))
         return p, q, pick(ar, br), pick(al, bl), pick(br, ar), pick(bl, al)
 
+    def choose(late, a, b):
+        if isinstance(a, tuple):
+            return tuple(choose(late, m, n) for m, n in zip(a, b))
+        return late * a + (1 - late) * b
+
     def copy(k, n, src, dst, dev):
         return pltpu.make_async_remote_copy(
             src_ref=src,
             dst_ref=dst,
-            send_sem=send_sem.at[k, SEND_SEM[n]],
+            send_sem=send_sem.at[SEND_SEM[n]],
             recv_sem=recv_sem.at[k, RECV_SEM[n]],
             device_id=dev,
             device_id_type=MESH,
@@ -261,7 +278,10 @@
         p, q, p_right, p_left, q_right, q_left = gather_places(k)
         p1, p3, q1, q3 = (p + 1) % 4, (p + 3) % 4, (q + 1) % 4, (q + 3) % 4
         same = lambda n, ref, dev: copy(k, n, ref, ref, dev)
-        near, far = pl.ds(0, 2), pl.ds(2, 2)
+        near, rest = pl.ds(0, 2), pl.ds(2, 2)
+        big = (k + CHUNKS - FAR_BIG) // CHUNKS
+        small = (k + CHUNKS - FAR_SMALL) // CHUNKS
+        far_big, far_small = far(k, 1), far(k, 0)
         return [
             lambda: copy(k, 0, terms.at[k, i2, 0], half_a.at[k, 0], ar),
             lambda: copy(k, 1, terms.at[k, i2, 1], half_a.at[k, 1], al),
@@ -275,23 +295,19 @@
             lambda: copy(k, 9, sums.at[k, j3], full_b.at[k, 1], bl),
             lambda: same(10, acts.at[k, p, q], q_right),
             lambda: same(11, acts.at[k, p, q], q_left),
-            lambda: same(12, acts.at[k, p, q3, 0], q_right),
-            lambda: same(13, acts.at[k, p, q1, 1], q_left),
+            lambda: same(12, acts.at[k, p, choose(small, q, q3), 0], choose(small, far_small, q_right)),
+            lambda: same(13, acts.at[k, p, choose(small, q, q1), 1], choose(small, far_small, q_left)),
             lambda: same(14, acts.at[k, p, near], p_right),
-            lambda: same(15, acts.at[k, p, far], p_left),
-            lambda: same(16, acts.at[k, p, far], p_right),
+            lambda: same(15, acts.at[k, p, rest], p_left),
+            lambda: same(16, acts.at[k, p, rest], p_right),
             lambda: same(17, acts.at[k, p, near], p_left),
-            lambda: same(18, acts.at[k, p3, near], p_right),
-            lambda: same(19, acts.at[k, p1, far], p_left),
+            lambda: same(18, acts.at[k, choose(big, p, p3), near], choose(big, far_big, p_right)),
+            lambda: same(19, acts.at[k, choose(big, p, p1), rest], choose(big, far_big, p_left)),
         ]
 
     def arrived(k, n, ref):
         i, j, ar, al, br, bl = places(k)
         copy(k, n, ref, ref, ar).wait_recv()
-
-    def left_here(k, n, ref):
-        i, j, ar, al, br, bl = places(k)
-        copy(k, n, ref, ref, ar).wait_send()
 
     def plus(a, b):
         return (a.astype(F32) + b.astype(F32)).astype(BF16)
@@ -357,12 +373,20 @@
         copies[10]().start()
         copies[11]().start()
 
+        @pl.when(k >= FAR_SMALL)
+        def _():
+            copies[12]().start()
+            copies[13]().start()
+
     def p5(k):
         p, q, *_ = gather_places(k)
         copies = all_copies(k)
         arrived(k, 10, acts.at[k, p, pl.ds(0, 2)])
-        copies[12]().start()
-        copies[13]().start()
+
+        @pl.when(k < FAR_SMALL)
+        def _():
+            copies[12]().start()
+            copies[13]().start()
 
     def p6(k):
         p, q, *_ = gather_places(k)
@@ -371,12 +395,20 @@
         for n in range(14, 18):
             copies[n]().start()
 
+        @pl.when(k >= FAR_BIG)
+        def _():
+            copies[18]().start()
+            copies[19]().start()
+
     def p7(k):
         p, q, *_ = gather_places(k)
         copies = all_copies(k)
         arrived(k, 14, acts.at[k, 0])
-        copies[18]().start()
-        copies[19]().start()
+
+        @pl.when(k < FAR_BIG)
+        def _():
+            copies[18]().start()
+            copies[19]().start()
 
     def p8(k):
         p, q, *_ = gather_places(k)
@@ -402,9 +434,6 @@
         for b in range(2):
             pairs[2 * k + b, :, 0:BLOCK] = gate_cols[b]
             pairs[2 * k + b, :, BLOCK:] = up_cols[b]
-        left_here(k, 0, terms.at[k, pl.ds(0, 3)])
-        left_here(k, 6, terms.at[k, pl.ds(0, 3), 0])
-        left_here(k, 14, terms.at[k, pl.ds(0, 3)])
 
     def tick(t, carry):
         for phase, late in zip((p7, p6, p5, p4, p3, p2, p1, p0, p8), LAGS[7::-1] + LAGS[8:]):
@@ -465,38 +494,46 @@
             mine = totals[arr][at * 2 + core] + tail_core[at, arr].astype(F32)
             tail[at, arr] = mine.astype(BF16)
 
-    steps = [
-        last(4, tail.at[x2, 0], tail_h.at[0], right),
-        last(5, tail.at[x2, 1], tail_h.at[1], left),
-        last(6, tail.at[x1, 1], tail_f.at[0, 1], right),
-        last(7, tail.at[x3, 0], tail_f.at[1, 0], left),
-        last(8, tail.at[x1, 0], tail_f.at[0, 0], right),
-        last(9, tail.at[x3, 1], tail_f.at[1, 1], left),
-    ]
+    halves = (pl.ds(0, 16), pl.ds(16, 16))
+    steps = (
+        [last(4 + h, tail.at[x2, 0, rows], tail_h.at[0, rows], right) for h, rows in enumerate(halves)]
+        + [last(6 + h, tail.at[x2, 1, rows], tail_h.at[1, rows], left) for h, rows in enumerate(halves)]
+        + [
+            last(8, tail.at[x1, 1], tail_f.at[0, 1], right),
+            last(9, tail.at[x3, 0], tail_f.at[1, 0], left),
+        ]
+        + [last(10, tail.at[x1, 0, rows], tail_f.at[0, 0, rows], right) for rows in halves]
+        + [last(11, tail.at[x3, 1, rows], tail_f.at[1, 1, rows], left) for rows in halves]
+    )
     lax.fori_loop(0, 2, down_group, 0)
     both(0, x2)
-    steps[0].start()
-    steps[1].start()
+    for n in range(4):
+        steps[n].start()
     both(1, x1)
-    steps[2].start()
+    steps[4].start()
     both(2, x3)
-    steps[3].start()
+    steps[5].start()
     lax.fori_loop(2, 6, down_group, 0)
-    lax.fori_loop(0, 3, gate_group, 0)
-    steps[0].wait_recv()
-    tail[x1, 0] = plus(tail[x1, 0], tail_h[0])
-    steps[4].start()
-    steps[1].wait_recv()
-    tail[x3, 1] = plus(tail[x3, 1], tail_h[1])
-    steps[5].start()
-    lax.fori_loop(3, 6, gate_group, 0)
+    lax.fori_loop(0, 2, gate_group, 0)
+    for h, rows in enumerate(halves):
+        steps[h].wait_recv()
+        tail[x1, 0, rows] = plus(tail[x1, 0, rows], tail_h[0, rows])
+        steps[6 + h].start()
+        steps[2 + h].wait_recv()
+        tail[x3, 1, rows] = plus(tail[x3, 1, rows], tail_h[1, rows])
+        steps[8 + h].start()
+    lax.fori_loop(2, 6, gate_group, 0)
     cores[3].wait_recv()
-    last(6, tail_f, tail_f, right).wait_recv()
+    last(8, tail_f, tail_f, right).wait_recv()
     for arr in range(2):
         total = totals[arr][x0 * 2 + core] + tail_core[x0, arr].astype(F32)
         total = total + tail_f[0, arr].astype(F32) + tail_f[1, arr].astype(F32)
         layer_ref[arr] = total.astype(BF16)
 
+    most = terms.at[:, pl.ds(0, 3)]
+    copy(0, 0, most, most, right).wait_send()
+    copy(0, 6, terms.at[:, pl.ds(0, 3), 0], terms.at[:, pl.ds(0, 3), 0], right).wait_send()
+    copy(0, 14, most, most, right).wait_send()
     last(0, tail_out, tail_core, sibling).wait_send()
     last(4, tail.at[pl.ds(0, 3)], tail.at[pl.ds(0, 3)], right).wait_send()
     head(0, xs.at[pl.ds(0, 7)], xs.at[pl.ds(0, 7)], right).wait_send()
@@ -545,11 +582,11 @@
             pltpu.SMEM((2, 8, 128), jnp.int32),
             pltpu.SemaphoreType.DMA((6,)),
             pltpu.SemaphoreType.DMA((1,)),
-            pltpu.SemaphoreType.DMA((7,)),
-            pltpu.SemaphoreType.DMA((CHUNKS, 3)),
+            pltpu.SemaphoreType.DMA((9,)),
+            pltpu.SemaphoreType.DMA((3,)),
             pltpu.SemaphoreType.DMA((CHUNKS, 8)),
             pltpu.SemaphoreType.DMA((2,)),
-            pltpu.SemaphoreType.DMA((7,)),
+            pltpu.SemaphoreType.DMA((9,)),
         ],
         compiler_params=pltpu.CompilerParams(
             collective_id=0, has_side_effects=True, vmem_limit_bytes=51 * 2**20
@@ -562,8 +599,10 @@
     layer, gate, up, down, out_ref, gradx_ref, gate_out, up_out, down_out, sem
 ):
     pairs = ((gate, gate_out), (up, up_out), (down, down_out))
+    quarters = [pl.ds(q * (NB // 4), NB // 4) for q in range(4)]
     saves = [
-        pltpu.make_async_copy(here.at[pl.ds(0, NB)], out, sem.at[n])
+        pltpu.make_async_copy(here.at[rows], out.at[rows], sem.at[n, q])
+        for q, rows in enumerate(quarters)
         for n, (here, out) in enumerate(pairs)
     ]
     for save in saves:
@@ -584,7 +623,7 @@
         out_shape=(tokens, tokens, blocks, blocks, blocks),
         in_specs=[vmem] + [anywhere] * 3,
         out_specs=(vmem, vmem, anywhere, anywhere, anywhere),
-        scratch_shapes=[pltpu.SemaphoreType.DMA((3,))],
+        scratch_shapes=[pltpu.SemaphoreType.DMA((3, 4))],
         compiler_params=pltpu.CompilerParams(vmem_limit_bytes=16 * 2**20),
         name="save",
     )(layer, *grads)

time: 94.1 us -> 92.7 us (0.985)
  Pallas kernels: 92 us -> 90.6 us
    pallas_call x1, Pallas kernels: 87.6 us -> 86.3 us  [run_layer(): pl.pallas_call(layer_kernel, out_shape=(pltpu.VMEM((2, 32, WIDTH), BF16),...]
where the time goes in v4:
time: 92.7 us; the launch traced here: 92.6 us
  Pallas kernels  90.6 us (98%)
  between operations  1.93 us (2%)
    pallas_call x1, Pallas kernels, run_layer(): pl.pallas_call(layer_kernel, out_shape=(pltpu.VMEM((2, 32, WIDTH), BF16),...  86.3 us
    pallas_call x1, Pallas kernels, run_save(): pl.pallas_call(save_kernel, out_shape=(tokens, tokens, blocks, blocks, bl...  4.37 us

profile of v4, /device:TPU:1, one launch (start us, length us, event | category | flops | bytes accessed | tf_op | source)
XLA Modules:
  0.0 92.6 jit_solution(14689046076090094929)
XLA Ops:
  1.9 86.3 %layer.1 = (bf16[2,32,1024]{2,1,0:T(8,128)(2,1)S(1)}, bf16[97,128,128]{2,1,0:T(8,128)(2,1)S(1)}, bf16[97,128,128]{2,1,0:T(8,128)(2,1)S(1)}, bf16[97,128,128]{2,1,0:T(8,128)(2,1)S(1)}) custom-call(s32[1,1,96]{2,1,0:T(1,128)} %gate_slots.1, s32[1,1]{1,0:T(1,128)S(6)} %copy.14.gate_count, s32[1,1,96]{2,1,0:T(1,128)} %down_slots.1, s32[1,1]{1,0:T(1,128)S(6)} %copy.15.down_count, ...), custom_call_target="tpu_custom_call" | custom-call | tf_op jit(solution)/shard_map/layer/pallas_call | solution.py:548
  88.2 4.4 %save.1 = (bf16[32,1024]{1,0:T(8,128)(2,1)}, bf16[32,1024]{1,0:T(8,128)(2,1)}, bf16[96,128,128]{2,1,0:T(8,128)(2,1)}, bf16[96,128,128]{2,1,0:T(8,128)(2,1)}, bf16[96,128,128]{2,1,0:T(8,128)(2,1)}) custom-call(bf16[2,32,1024]{2,1,0:T(8,128)(2,1)S(1)} %get-tuple-element.14.layer, bf16[97,128,128]{2,1,0:T(8,128)(2,1)S(1)} %get-tuple-element.15.gate, ...), custom_call_target="tpu_custom_call" | custom-call | tf_op jit(solution)/shard_map/save/pallas_call | solution.py:621

commit v5 on v4

--- a/solution.py
+++ b/solution.py
@@ -14,7 +14,6 @@
 CHUNK = 2 * BLOCK
 CHUNKS = FPB // 2
 GROUP = 16
-FAR_BIG, FAR_SMALL = 13, 13
 LAGS = (0, 4, 8, 12, 16, 20, 24, 28, 32)
 MESH = pl.DeviceIdType.MESH
 TAIL_SEND = (0,) * 4 + (1,) * 8
@@ -231,7 +230,7 @@
             cots[r] = xs[:, 1, :, cols].reshape(TOKENS, BLOCK)
 
     def places(k):
-        odd = k % 2
+        odd = (k + core) % 2
         i = (1 - odd) * y + odd * z
         j = (1 - odd) * z + odd * y
 
@@ -241,25 +240,6 @@
             return (z_new * 4 + y_new, col)
 
         return i, j, dev(1, odd), dev(3, odd), dev(1, 1 - odd), dev(3, 1 - odd)
-
-    def far(k, along_a):
-        along_z = swap(k, k % 2, 1 - k % 2)[1 - along_a]
-        return ((z + 2 * along_z) % 4 * 4 + (y + 2 * (1 - along_z)) % 4, col)
-
-    def swap(k, a, b):
-        turned = k // (CHUNKS - 1)
-        return (1 - turned) * a + turned * b, (1 - turned) * b + turned * a
-
-    def gather_places(k):
-        i, j, ar, al, br, bl = places(k)
-        p, q = swap(k, i, j)
-        pick = lambda a, b: tuple(swap(k, m, n)[0] for m, n in zip(a, b))
-        return p, q, pick(ar, br), pick(al, bl), pick(br, ar), pick(bl, al)
-
-    def choose(late, a, b):
-        if isinstance(a, tuple):
-            return tuple(choose(late, m, n) for m, n in zip(a, b))
-        return late * a + (1 - late) * b
 
     def copy(k, n, src, dst, dev):
         return pltpu.make_async_remote_copy(
@@ -275,13 +255,8 @@
         i, j, ar, al, br, bl = places(k)
         i1, i2, i3 = (i + 1) % 4, (i + 2) % 4, (i + 3) % 4
         j1, j2, j3 = (j + 1) % 4, (j + 2) % 4, (j + 3) % 4
-        p, q, p_right, p_left, q_right, q_left = gather_places(k)
-        p1, p3, q1, q3 = (p + 1) % 4, (p + 3) % 4, (q + 1) % 4, (q + 3) % 4
         same = lambda n, ref, dev: copy(k, n, ref, ref, dev)
         near, rest = pl.ds(0, 2), pl.ds(2, 2)
-        big = (k + CHUNKS - FAR_BIG) // CHUNKS
-        small = (k + CHUNKS - FAR_SMALL) // CHUNKS
-        far_big, far_small = far(k, 1), far(k, 0)
         return [
             lambda: copy(k, 0, terms.at[k, i2, 0], half_a.at[k, 0], ar),
             lambda: copy(k, 1, terms.at[k, i2, 1], half_a.at[k, 1], al),
@@ -293,16 +268,16 @@
             lambda: copy(k, 7, sums.at[k, j2, 1], half_b.at[k, 1], bl),
             lambda: copy(k, 8, sums.at[k, j1], full_b.at[k, 0], br),
             lambda: copy(k, 9, sums.at[k, j3], full_b.at[k, 1], bl),
-            lambda: same(10, acts.at[k, p, q], q_right),
-            lambda: same(11, acts.at[k, p, q], q_left),
-            lambda: same(12, acts.at[k, p, choose(small, q, q3), 0], choose(small, far_small, q_right)),
-            lambda: same(13, acts.at[k, p, choose(small, q, q1), 1], choose(small, far_small, q_left)),
-            lambda: same(14, acts.at[k, p, near], p_right),
-            lambda: same(15, acts.at[k, p, rest], p_left),
-            lambda: same(16, acts.at[k, p, rest], p_right),
-            lambda: same(17, acts.at[k, p, near], p_left),
-            lambda: same(18, acts.at[k, choose(big, p, p3), near], choose(big, far_big, p_right)),
-            lambda: same(19, acts.at[k, choose(big, p, p1), rest], choose(big, far_big, p_left)),
+            lambda: same(10, acts.at[k, i, j], br),
+            lambda: same(11, acts.at[k, i, j], bl),
+            lambda: same(12, acts.at[k, i, j3, 0], br),
+            lambda: same(13, acts.at[k, i, j1, 1], bl),
+            lambda: same(14, acts.at[k, i, near], ar),
+            lambda: same(15, acts.at[k, i, rest], al),
+            lambda: same(16, acts.at[k, i, rest], ar),
+            lambda: same(17, acts.at[k, i, near], al),
+            lambda: same(18, acts.at[k, i3, near], ar),
+            lambda: same(19, acts.at[k, i1, rest], al),
         ]
 
     def arrived(k, n, ref):
@@ -361,64 +336,45 @@
 
     def p4(k):
         i, j, *_ = places(k)
-        p, q, *_ = gather_places(k)
         copies = all_copies(k)
         arrived(k, 8, full_b.at[k])
         total = sums[k, j].astype(F32) + full_b[k, 0].astype(F32) + full_b[k, 1].astype(F32)
         gate, up, grad = total[:, 0:16], total[:, 16:32], total[:, 32:48]
         sigma = 1.0 / (1.0 + jnp.exp(-gate))
-        acts[k, p, q, :, 0:16, :] = (gate * sigma * up).astype(BF16)
-        acts[k, p, q, :, 16:32, :] = (grad * up * sigma * (1.0 + gate * (1.0 - sigma))).astype(BF16)
-        acts[k, p, q, :, 32:48, :] = (grad * gate * sigma).astype(BF16)
+        acts[k, i, j, :, 0:16, :] = (gate * sigma * up).astype(BF16)
+        acts[k, i, j, :, 16:32, :] = (grad * up * sigma * (1.0 + gate * (1.0 - sigma))).astype(BF16)
+        acts[k, i, j, :, 32:48, :] = (grad * gate * sigma).astype(BF16)
         copies[10]().start()
         copies[11]().start()
 
-        @pl.when(k >= FAR_SMALL)
-        def _():
-            copies[12]().start()
-            copies[13]().start()
-
     def p5(k):
-        p, q, *_ = gather_places(k)
-        copies = all_copies(k)
-        arrived(k, 10, acts.at[k, p, pl.ds(0, 2)])
-
-        @pl.when(k < FAR_SMALL)
-        def _():
-            copies[12]().start()
-            copies[13]().start()
+        i, j, *_ = places(k)
+        copies = all_copies(k)
+        arrived(k, 10, acts.at[k, i, pl.ds(0, 2)])
+        copies[12]().start()
+        copies[13]().start()
 
     def p6(k):
-        p, q, *_ = gather_places(k)
-        copies = all_copies(k)
-        arrived(k, 12, acts.at[k, p, 0])
+        i, j, *_ = places(k)
+        copies = all_copies(k)
+        arrived(k, 12, acts.at[k, i, 0])
         for n in range(14, 18):
             copies[n]().start()
 
-        @pl.when(k >= FAR_BIG)
-        def _():
-            copies[18]().start()
-            copies[19]().start()
-
     def p7(k):
-        p, q, *_ = gather_places(k)
+        i, j, *_ = places(k)
         copies = all_copies(k)
         arrived(k, 14, acts.at[k, 0])
-
-        @pl.when(k < FAR_BIG)
-        def _():
-            copies[18]().start()
-            copies[19]().start()
+        copies[18]().start()
+        copies[19]().start()
 
     def p8(k):
-        p, q, *_ = gather_places(k)
+        i, j, *_ = places(k)
         arrived(k, 16, acts.at[k, pl.ds(0, 2)])
-
-        groups = [swap(k, a, b) for a in range(4) for b in range(4)]
 
         def act(part):
             cols = [
-                jnp.concatenate([acts[k, u, v, b, part * 16 : (part + 1) * 16, :] for u, v in groups])
+                acts[k, :, :, b, part * 16 : (part + 1) * 16, :].reshape(TOKENS, BLOCK)
                 for b in range(2)
             ]
             return cols, jnp.concatenate(cols, axis=1)

time: 92.7 us -> 92.4 us (level)
  no operation moved by 1% of the time
where the time goes in v5:
time: 92.4 us; the launch traced here: 92.3 us
  Pallas kernels  90.4 us (98%)
  between operations  1.93 us (2%)
    pallas_call x1, Pallas kernels, run_layer(): pl.pallas_call(layer_kernel, out_shape=(pltpu.VMEM((2, 32, WIDTH), BF16),...  86 us
    pallas_call x1, Pallas kernels, run_save(): pl.pallas_call(save_kernel, out_shape=(tokens, tokens, blocks, blocks, bl...  4.37 us

profile of v5, /device:TPU:1, one launch (start us, length us, event | category | flops | bytes accessed | tf_op | source)
XLA Modules:
  0.0 92.3 jit_solution(2464359871457619915)
XLA Ops:
  1.9 86.0 %layer.1 = (bf16[2,32,1024]{2,1,0:T(8,128)(2,1)S(1)}, bf16[97,128,128]{2,1,0:T(8,128)(2,1)S(1)}, bf16[97,128,128]{2,1,0:T(8,128)(2,1)S(1)}, bf16[97,128,128]{2,1,0:T(8,128)(2,1)S(1)}) custom-call(s32[1,1,96]{2,1,0:T(1,128)} %gate_slots.1, s32[1,1]{1,0:T(1,128)S(6)} %copy.14.gate_count, s32[1,1,96]{2,1,0:T(1,128)} %down_slots.1, s32[1,1]{1,0:T(1,128)S(6)} %copy.15.down_count, ...), custom_call_target="tpu_custom_call" | custom-call | tf_op jit(solution)/shard_map/layer/pallas_call | solution.py:504
  87.9 4.4 %save.1 = (bf16[32,1024]{1,0:T(8,128)(2,1)}, bf16[32,1024]{1,0:T(8,128)(2,1)}, bf16[96,128,128]{2,1,0:T(8,128)(2,1)}, bf16[96,128,128]{2,1,0:T(8,128)(2,1)}, bf16[96,128,128]{2,1,0:T(8,128)(2,1)}) custom-call(bf16[2,32,1024]{2,1,0:T(8,128)(2,1)S(1)} %get-tuple-element.14.layer, bf16[97,128,128]{2,1,0:T(8,128)(2,1)S(1)} %get-tuple-element.15.gate, ...), custom_call_target="tpu_custom_call" | custom-call | tf_op jit(solution)/shard_map/save/pallas_call | solution.py:577

commit v6 on v5

--- a/solution.py
+++ b/solution.py
@@ -14,7 +14,7 @@
 CHUNK = 2 * BLOCK
 CHUNKS = FPB // 2
 GROUP = 16
-LAGS = (0, 4, 8, 12, 16, 20, 24, 28, 32)
+LAGS = (0, 5, 10, 15, 20, 25, 30, 35, 40)
 MESH = pl.DeviceIdType.MESH
 TAIL_SEND = (0,) * 4 + (1,) * 8
 TAIL_RECV = tuple(range(8)) + (8,) * 4

time: 92.4 us -> 92.6 us (level)
  no operation moved by 1% of the time
where the time goes in v6:
time: 92.6 us; the launch traced here: 92.4 us
  Pallas kernels  90.5 us (98%)
  between operations  1.93 us (2%)
    pallas_call x1, Pallas kernels, run_layer(): pl.pallas_call(layer_kernel, out_shape=(pltpu.VMEM((2, 32, WIDTH), BF16),...  86.1 us
    pallas_call x1, Pallas kernels, run_save(): pl.pallas_call(save_kernel, out_shape=(tokens, tokens, blocks, blocks, bl...  4.37 us

profile of v6, /device:TPU:1, one launch (start us, length us, event | category | flops | bytes accessed | tf_op | source)
XLA Modules:
  0.0 92.4 jit_solution(6561906703175225905)
XLA Ops:
  1.9 86.1 %layer.1 = (bf16[2,32,1024]{2,1,0:T(8,128)(2,1)S(1)}, bf16[97,128,128]{2,1,0:T(8,128)(2,1)S(1)}, bf16[97,128,128]{2,1,0:T(8,128)(2,1)S(1)}, bf16[97,128,128]{2,1,0:T(8,128)(2,1)S(1)}) custom-call(s32[1,1,96]{2,1,0:T(1,128)} %gate_slots.1, s32[1,1]{1,0:T(1,128)S(6)} %copy.14.gate_count, s32[1,1,96]{2,1,0:T(1,128)} %down_slots.1, s32[1,1]{1,0:T(1,128)S(6)} %copy.15.down_count, ...), custom_call_target="tpu_custom_call" | custom-call | tf_op jit(solution)/shard_map/layer/pallas_call | solution.py:504
  88.1 4.4 %save.1 = (bf16[32,1024]{1,0:T(8,128)(2,1)}, bf16[32,1024]{1,0:T(8,128)(2,1)}, bf16[96,128,128]{2,1,0:T(8,128)(2,1)}, bf16[96,128,128]{2,1,0:T(8,128)(2,1)}, bf16[96,128,128]{2,1,0:T(8,128)(2,1)}) custom-call(bf16[2,32,1024]{2,1,0:T(8,128)(2,1)S(1)} %get-tuple-element.14.layer, bf16[97,128,128]{2,1,0:T(8,128)(2,1)S(1)} %get-tuple-element.15.gate, ...), custom_call_target="tpu_custom_call" | custom-call | tf_op jit(solution)/shard_map/save/pallas_call | solution.py:577
